TPU v7x, 256 devices: a whole 4x4x8 slice. The times are simulated.
256 devices in a mesh: chain: 16 (over z, core), tile: 16 (over y, x).
Axes of the slice: x: 4, y: 4, z: 8, core: 2. Of those that a mesh axis runs over, the one named last changes fastest.
Arguments:
- inverse_diag: bfloat16 [32, 768, 768], P('chain', 'tile'), as said below
- sub_diag: bfloat16 [32, 768, 768], P('chain', 'tile')
- arrow_rows: bfloat16 [32, 128, 768], P('chain', 'tile'), may hold values from -0.3125 to 0.3125
- arrow_inverse: bfloat16 [128, 128], replicated, as said below
Outputs:
- diag_inverse: float32 [32, 768, 768], P('chain', 'tile')
- arrow_blocks: float32 [32, 128, 768], P('chain', 'tile')
Inputs may be any that keep to these rules, and one draw needn't show every extreme that they name: `inverse_diag`: every block is lower triangular with a positive diagonal. `arrow_inverse`: lower triangular with a positive diagonal.
All inputs are finite; a program needn't handle non-finite values.
Results may differ from a plain program's by a relative error of at most 0.019.
Values may be sent and summed in bfloat16 or wider, within the bound.
A program may use at most 64 MiB of HBM per device.

v0:
```python
import jax
import jax.numpy as jnp
from jax import lax
from jax.sharding import PartitionSpec as P


def shifted(value, axis, steps):
    count = lax.axis_size(axis)
    first, last = (max(0, -steps), min(count, count - steps))
    return lax.ppermute(value, axis, [(source, source + steps) for source in range(first, last)])


def transposed_dot(left_part, right_part, precision=None):
    return lax.dot_general(
        left_part,
        right_part,
        (((0,), (0,)), ((), ())),
        precision=precision,
        preferred_element_type=jnp.float32,
    )


def plain_dot(left_part, right_part):
    return jnp.dot(left_part, right_part, preferred_element_type=jnp.float32)


def congruence(left_full, right_rows, out_rows):
    right_full = lax.all_gather(right_rows, "tile", axis=0, tiled=True)
    columns = lax.dynamic_slice_in_dim(left_full, lax.axis_index("tile") * out_rows, out_rows, 1)
    return transposed_dot(columns, right_full)


def compose(near_full, near_arrow, near_diag, far_main, far_arrow, far_diag):
    new_main = plain_dot(far_main, near_full)
    new_arrow = plain_dot(far_arrow, near_full) + near_arrow
    carried = plain_dot(far_diag, near_full).astype(jnp.bfloat16)
    new_diag = congruence(near_full, carried, near_diag.shape[0]) + near_diag
    return (new_main, new_arrow, new_diag)


def on_device(inverse_diag, sub_diag, arrow_rows, arrow_inverse):
    block_count, row_count, node_count = inverse_diag.shape
    arrow_count = arrow_rows.shape[1]
    tile_count = lax.axis_size("tile")
    chain_count = lax.axis_size("chain")
    own_offset = lax.axis_index("tile") * row_count
    arrow_offset = lax.axis_index("tile") * arrow_count
    highest = lax.Precision.HIGHEST
    shard_rows = lax.all_gather(inverse_diag, "tile", axis=1, tiled=True)
    own_cols = lax.dynamic_slice_in_dim(shard_rows, own_offset, row_count, 2)
    coupling_sum = jnp.einsum(
        "kij,kjl->kil", sub_diag, shard_rows, preferred_element_type=jnp.float32
    )
    arrow_sum = jnp.einsum(
        "kij,kjl->kil", arrow_rows, shard_rows, preferred_element_type=jnp.float32
    )
    square_sum = jnp.einsum(
        "kji,kjl->kil", own_cols, shard_rows, preferred_element_type=jnp.float32
    )
    coupling_rows = coupling_sum
    arrow_map_rows = arrow_sum
    coupling_rows = coupling_rows.astype(jnp.bfloat16)
    arrow_map_rows = arrow_map_rows.astype(jnp.bfloat16)
    coupling_full, arrow_map_full = (
        lax.all_gather(coupling_rows, "tile", axis=1, tiled=True),
        lax.all_gather(arrow_map_rows, "tile", axis=1, tiled=True),
    )
    main = -coupling_rows[block_count - 1].astype(jnp.float32)
    arrow_state = -arrow_map_rows[block_count - 1].astype(jnp.float32)
    diag_state = square_sum[block_count - 1]
    block_index = 0
    main, arrow_state, diag_state = compose(
        -coupling_full[block_index],
        -arrow_map_rows[block_index].astype(jnp.float32),
        square_sum[block_index],
        main.astype(jnp.bfloat16),
        arrow_state.astype(jnp.bfloat16),
        diag_state.astype(jnp.bfloat16),
    )
    position = lax.axis_index("chain")
    for section_index in range((chain_count - 1).bit_length()):
        distance = 1 << section_index
        near_full = lax.all_gather(main.astype(jnp.bfloat16), "tile", axis=0, tiled=True)
        packed = jnp.concatenate([main, diag_state, arrow_state], axis=0).astype(jnp.bfloat16)
        arrived = shifted(packed, "chain", -distance)
        far_main = arrived[:row_count]
        far_diag = arrived[row_count : 2 * row_count]
        far_arrow = arrived[2 * row_count :]
        updated = compose(near_full, arrow_state, diag_state, far_main, far_arrow, far_diag)
        receives = position + distance < chain_count
        main = jnp.where(receives, updated[0], main)
        arrow_state = jnp.where(receives, updated[1], arrow_state)
        diag_state = jnp.where(receives, updated[2], diag_state)
    sigma_aa = transposed_dot(arrow_inverse, arrow_inverse)
    arrow_whole = lax.all_gather(arrow_state, "tile", axis=0, tiled=True)
    boundary_arrow = jnp.dot(sigma_aa, arrow_whole, precision=highest)
    columns = lax.dynamic_slice_in_dim(arrow_whole, own_offset, row_count, 1)
    first_diag = transposed_dot(columns, boundary_arrow, highest) + diag_state
    first_arrow = lax.dynamic_slice_in_dim(boundary_arrow, arrow_offset, arrow_count, 0)
    diag_blocks = [first_diag] * block_count
    arrow_blocks = [first_arrow] * block_count
    arrived = shifted(
        jnp.concatenate([first_diag, first_arrow], axis=0).astype(jnp.bfloat16), "chain", -1
    ).astype(jnp.float32)
    state_diag = arrived[:row_count]
    state_arrow = arrived[row_count:]
    sigma_rows = lax.dynamic_slice_in_dim(sigma_aa, arrow_offset, arrow_count, 0).astype(
        jnp.bfloat16
    )
    block_index = 1
    arrow_gathered = lax.all_gather(state_arrow, "tile", axis=0, tiled=True)
    arrow_columns = lax.dynamic_slice_in_dim(arrow_gathered, own_offset, row_count, 1)
    coupling_block = coupling_full[block_index]
    arrow_block = arrow_map_full[block_index]
    w_first = plain_dot(state_diag.astype(jnp.bfloat16), coupling_block) + transposed_dot(
        arrow_columns.astype(jnp.bfloat16), arrow_block
    )
    w_second = plain_dot(state_arrow.astype(jnp.bfloat16), coupling_block) + plain_dot(
        sigma_rows, arrow_block
    )
    arranged = jnp.concatenate(
        [
            coupling_block.reshape(tile_count, row_count, node_count),
            arrow_block.reshape(tile_count, arrow_count, node_count),
        ],
        axis=1,
    ).reshape(-1, node_count)
    right_rows = jnp.concatenate([w_first, w_second], axis=0).astype(jnp.bfloat16)
    state_diag = square_sum[block_index] + congruence(arranged, right_rows, row_count)
    state_arrow = -w_second
    diag_blocks[block_index] = state_diag
    arrow_blocks[block_index] = state_arrow
    return (jnp.stack(diag_blocks), jnp.stack(arrow_blocks))


def solution(mesh):
    placed = (P("chain", "tile", None), P("chain", "tile", None), P("chain", "tile", None), P())
    return jax.shard_map(
        on_device,
        mesh=mesh,
        in_specs=placed,
        out_specs=(P("chain", "tile", None), P("chain", "tile", None)),
        check_vma=False,
    )
```

profile of v0, /device:TPU:32, one launch (start us, length us, event | category | flops | bytes accessed | tf_op | source)
XLA Modules:
  0.0 655.0 jit_solution(7171459305833535482)
XLA Ops:
  8.0 55.9 %all-gather.13.cloned.1.call-done = bf16[2,768,768]{2,1,0:T(8,128)(2,1)} async-done(((bf16[2,48,768]{2,1,0:T(8,128)(2,1)}), bf16[2,768,768]{2,1,0:T(8,128)(2,1)}) %all-gather.13.cloned.1.call-update) | async-done | bytes 2359312 | tf_op jit(solution)/shard_map/all_gather | solution.py:49
  63.9 3.0 convolution_convert_fusion
  67.7 49.5 %all-gather.15.cloned.1.call-done = bf16[2,768,768]{2,1,0:T(8,128)(2,1)} async-done(((bf16[2,48,768]{2,1,0:T(8,128)(2,1)}), bf16[2,768,768]{2,1,0:T(8,128)(2,1)}) %all-gather.15.cloned.1.call-update) | async-done | bytes 2359312 | tf_op jit(solution)/shard_map/all_gather | solution.py:65
  117.2 2.2 fusion.18
  119.5 2.2 fusion.8
  123.9 43.1 %all-gather.17.cloned.1.call-done = bf16[768,768]{1,0:T(8,128)(2,1)} async-done(((bf16[48,768]{1,0:T(8,128)(2,1)}), bf16[768,768]{1,0:T(8,128)(2,1)}) %all-gather.17.cloned.1.call-update) | async-done | bytes 1179664 | tf_op jit(solution)/shard_map/all_gather | solution.py:28
  167.1 1.8 fusion.85
  168.8 1.9 collective-permute-start
  170.8 46.1 %all-gather.19.cloned.1.call-done = bf16[768,768]{1,0:T(8,128)(2,1)} async-done(((bf16[48,768]{1,0:T(8,128)(2,1)}), bf16[768,768]{1,0:T(8,128)(2,1)}) %all-gather.19.cloned.1.call-update) | async-done | bytes 1179664 | tf_op jit(solution)/shard_map/all_gather | solution.py:83
  216.9 2.3 convolution_convert_fusion.4
  220.6 46.3 %all-gather.21.cloned.1.call-done = bf16[768,768]{1,0:T(8,128)(2,1)} async-done(((bf16[48,768]{1,0:T(8,128)(2,1)}), bf16[768,768]{1,0:T(8,128)(2,1)}) %all-gather.21.cloned.1.call-update) | async-done | bytes 1179664 | tf_op jit(solution)/shard_map/all_gather | solution.py:28
  266.9 1.8 fusion.87
  268.7 2.4 collective-permute-start.1
  271.1 45.7 %all-gather.23.cloned.1.call-done = bf16[768,768]{1,0:T(8,128)(2,1)} async-done(((bf16[48,768]{1,0:T(8,128)(2,1)}), bf16[768,768]{1,0:T(8,128)(2,1)}) %all-gather.23.cloned.1.call-update) | async-done | bytes 1179664 | tf_op jit(solution)/shard_map/all_gather | solution.py:83
  316.8 2.3 convolution_convert_fusion.3
  320.5 46.3 %all-gather.25.cloned.1.call-done = bf16[768,768]{1,0:T(8,128)(2,1)} async-done(((bf16[48,768]{1,0:T(8,128)(2,1)}), bf16[768,768]{1,0:T(8,128)(2,1)}) %all-gather.25.cloned.1.call-update) | async-done | bytes 1179664 | tf_op jit(solution)/shard_map/all_gather | solution.py:28
  366.8 1.8 fusion.89
  369.9 46.9 %all-gather.27.cloned.1.call-done = bf16[768,768]{1,0:T(8,128)(2,1)} async-done(((bf16[48,768]{1,0:T(8,128)(2,1)}), bf16[768,768]{1,0:T(8,128)(2,1)}) %all-gather.27.cloned.1.call-update) | async-done | bytes 1179664 | tf_op jit(solution)/shard_map/all_gather | solution.py:83
  416.8 2.3 convolution_convert_fusion.2
  420.6 46.3 %all-gather.29.cloned.1.call-done = bf16[768,768]{1,0:T(8,128)(2,1)} async-done(((bf16[48,768]{1,0:T(8,128)(2,1)}), bf16[768,768]{1,0:T(8,128)(2,1)}) %all-gather.29.cloned.1.call-update) | async-done | bytes 1179664 | tf_op jit(solution)/shard_map/all_gather | solution.py:28
  466.9 1.8 fusion.91
  468.7 1.3 collective-permute-start.3
  470.0 46.7 %all-gather.31.cloned.1.call-done = bf16[768,768]{1,0:T(8,128)(2,1)} async-done(((bf16[48,768]{1,0:T(8,128)(2,1)}), bf16[768,768]{1,0:T(8,128)(2,1)}) %all-gather.31.cloned.1.call-update) | async-done | bytes 1179664 | tf_op jit(solution)/shard_map/all_gather | solution.py:83
  516.7 2.3 convolution_convert_fusion.1
  519.3 23.5 %all_gather.57 = bf16[2,128,768]{2,1,0:T(8,128)(2,1)S(1)} all-gather(bf16[2,8,768]{2,1,0:T(8,128)(2,1)S(1)} %convolution_convert_fusion.5), channel_id=1, replica_groups=mesh['chain'=16,'tile'=16] {'tile'}, dimensions={1}, use_global_device_ids=true | all-gather | bytes 417792 | tf_op jit(solution)/shard_map/all_gather | solution.py:66
  543.1 22.2 %all_gather.55 = f32[128,768]{1,0:T(8,128)S(1)} all-gather(f32[8,768]{1,0:T(8,128)S(1)} %fusion.31), channel_id=1, replica_groups=mesh['chain'=16,'tile'=16] {'tile'}, dimensions={0}, use_global_device_ids=true | all-gather | bytes 417792 | tf_op jit(solution)/shard_map/all_gather | solution.py:95
  567.0 1.9 fusion.14
  569.4 1.9 collective-permute-start.4
  571.5 1.9 collective-permute-done.4
  573.4 23.2 %all_gather.58 = bf16[128,768]{1,0:T(8,128)(2,1)S(1)} all-gather(bf16[8,768]{1,0:T(8,128)(2,1)S(1)} %slice.183), channel_id=1, replica_groups=mesh['chain'=16,'tile'=16] {'tile'}, dimensions={0}, use_global_device_ids=true | all-gather | bytes 208896 | tf_op jit(solution)/shard_map/all_gather | solution.py:111
  600.8 44.6 %all-gather.35.cloned.1.call-done = bf16[896,768]{1,0:T(8,128)(2,1)} async-done(((bf16[56,768]{1,0:T(8,128)(2,1)}), bf16[896,768]{1,0:T(8,128)(2,1)}) %all-gather.35.cloned.1.call-update) | async-done | bytes 1376272 | tf_op jit(solution)/shard_map/all_gather | solution.py:28
  645.4 2.0 fusion.13
  (99 shorter events, 16.9 us)
Async XLA Ops:
  7.2 56.7 %copy-start = (bf16[2,48,768]{2,1,0:T(8,128)(2,1)S(1)}, bf16[2,48,768]{2,1,0:T(8,128)(2,1)}, u32[]{:S(2)}) copy-start(bf16[2,48,768]{2,1,0:T(8,128)(2,1)} %param.5) | copy-start | bytes 442372
  7.2 56.7 %all-gather.13.cloned.1.call-start = ((), (), s32[]{:S(2)}) async-start(), calls=%async_computation | async-start | bytes 2506752 | tf_op jit(solution)/shard_map/all_gather | solution.py:49
  7.9 109.3 %all-gather.15.cloned.1.call-start = ((), (), s32[]{:S(2)}) async-start(), calls=%async_computation.1 | async-start | bytes 2506752 | tf_op jit(solution)/shard_map/all_gather | solution.py:65
  63.9 3.1 copy-start.1
  66.9 100.1 %all-gather.17.cloned.1.call-start = ((), (), s32[]{:S(2)}) async-start(), calls=%async_computation.2 | async-start | bytes 1253376 | tf_op jit(solution)/shard_map/all_gather | solution.py:28
  67.7 99.4 %copy-start.12 = (f32[2,48,768]{2,1,0:T(8,128)}, f32[2,48,768]{2,1,0:T(8,128)S(1)}, u32[]{:S(2)}) copy-start(f32[2,48,768]{2,1,0:T(8,128)S(1)} %fusion.35) | copy-start | bytes 884740
  67.7 51.8 %copy-start.16 = (bf16[2,48,768]{2,1,0:T(8,128)(2,1)S(1)}, bf16[2,48,768]{2,1,0:T(8,128)(2,1)}, u32[]{:S(2)}) copy-start(bf16[2,48,768]{2,1,0:T(8,128)(2,1)} %convolution_convert_fusion) | copy-start | bytes 442372
  119.4 97.5 %all-gather.19.cloned.1.call-start = ((), (), s32[]{:S(2)}) async-start(), calls=%async_computation.3 | async-start | bytes 1253376 | tf_op jit(solution)/shard_map/all_gather | solution.py:83
  121.7 145.2 %all-gather.21.cloned.1.call-start = ((), (), s32[]{:S(2)}) async-start(), calls=%async_computation.4 | async-start | bytes 1253376 | tf_op jit(solution)/shard_map/all_gather | solution.py:28
  123.9 44.9 %copy-start.14 = (bf16[48,768]{1,0:T(8,128)(2,1)S(1)}, bf16[48,768]{1,0:T(8,128)(2,1)}, u32[]{:S(2)}) copy-start(bf16[48,768]{1,0:T(8,128)(2,1)} %fusion.8) | copy-start | bytes 221188
  168.8 48.1 %collective-permute-start = (bf16[104,768]{1,0:T(8,128)(2,1)S(1)}, bf16[104,768]{1,0:T(8,128)(2,1)S(1)}, u32[]{:S(2)}, u32[]{:S(2)}) collective-permute-start(bf16[104,768]{1,0:T(8,128)(2,1)S(1)} %pad_maximum_fusion.2), channel_id=1, source_target_pairs={{16,0},{32,16},{48,32},{64,48},{80,64},{96,80},{112,96},{128,112},... | collective-permute-start | bytes 479240 | tf_op jit(solution)/shard_map/ppermute | solution.py:10
  216.9 2.4 copy-start.2
  219.3 97.5 %all-gather.23.cloned.1.call-start = ((), (), s32[]{:S(2)}) async-start(), calls=%async_computation.5 | async-start | bytes 1253376 | tf_op jit(solution)/shard_map/all_gather | solution.py:83
  220.3 146.5 %all-gather.25.cloned.1.call-start = ((), (), s32[]{:S(2)}) async-start(), calls=%async_computation.6 | async-start | bytes 1253376 | tf_op jit(solution)/shard_map/all_gather | solution.py:28
  220.6 48.1 %copy-start.10 = (bf16[48,768]{1,0:T(8,128)(2,1)S(1)}, bf16[48,768]{1,0:T(8,128)(2,1)}, u32[]{:S(2)}) copy-start(bf16[48,768]{1,0:T(8,128)(2,1)} %convolution_select_fusion.2) | copy-start | bytes 221188
  268.7 48.1 %collective-permute-start.1 = (bf16[104,768]{1,0:T(8,128)(2,1)S(1)}, bf16[104,768]{1,0:T(8,128)(2,1)S(1)}, u32[]{:S(2)}, u32[]{:S(2)}) collective-permute-start(bf16[104,768]{1,0:T(8,128)(2,1)S(1)} %pad_maximum_fusion.3), channel_id=1, source_target_pairs={{32,0},{48,16},{64,32},{80,48},{96,64},{112,80},{128,96},{144,112}... | collective-permute-start | bytes 479240 | tf_op jit(solution)/shard_map/ppermute | solution.py:10
  316.8 2.4 copy-start.3
  319.2 97.7 %all-gather.27.cloned.1.call-start = ((), (), s32[]{:S(2)}) async-start(), calls=%async_computation.7 | async-start | bytes 1253376 | tf_op jit(solution)/shard_map/all_gather | solution.py:83
  320.2 146.7 %all-gather.29.cloned.1.call-start = ((), (), s32[]{:S(2)}) async-start(), calls=%async_computation.8 | async-start | bytes 1253376 | tf_op jit(solution)/shard_map/all_gather | solution.py:28
  320.5 48.1 %copy-start.11 = (bf16[48,768]{1,0:T(8,128)(2,1)S(1)}, bf16[48,768]{1,0:T(8,128)(2,1)}, u32[]{:S(2)}) copy-start(bf16[48,768]{1,0:T(8,128)(2,1)} %convolution_select_fusion.1) | copy-start | bytes 221188
  368.6 48.2 %collective-permute-start.2 = (bf16[104,768]{1,0:T(8,128)(2,1)S(1)}, bf16[104,768]{1,0:T(8,128)(2,1)S(1)}, u32[]{:S(2)}, u32[]{:S(2)}) collective-permute-start(bf16[104,768]{1,0:T(8,128)(2,1)S(1)} %pad_maximum_fusion.4), channel_id=1, source_target_pairs={{64,0},{80,16},{96,32},{112,48},{128,64},{144,80},{160,96},{176,11... | collective-permute-start | bytes 479240 | tf_op jit(solution)/shard_map/ppermute | solution.py:10
  416.8 2.4 copy-start.4
  419.2 97.5 %all-gather.31.cloned.1.call-start = ((), (), s32[]{:S(2)}) async-start(), calls=%async_computation.9 | async-start | bytes 1253376 | tf_op jit(solution)/shard_map/all_gather | solution.py:83
  420.2 146.8 %all-gather.33.cloned.1.call-start = ((), (), s32[]{:S(2)}) async-start(), calls=%async_computation.10 | async-start | bytes 1253376 | tf_op jit(solution)/shard_map/all_gather | solution.py:28
  420.6 48.1 %copy-start.15 = (bf16[48,768]{1,0:T(8,128)(2,1)S(1)}, bf16[48,768]{1,0:T(8,128)(2,1)}, u32[]{:S(2)}) copy-start(bf16[48,768]{1,0:T(8,128)(2,1)} %fusion.21) | copy-start | bytes 221188
  468.6 50.5 %copy-start.17 = (bf16[128,128]{1,0:T(8,128)(2,1)S(1)}, bf16[128,128]{1,0:T(8,128)(2,1)}, u32[]{:S(2)}) copy-start(bf16[128,128]{1,0:T(8,128)(2,1)} %param.7) | copy-start | bytes 98308
  468.7 48.0 %collective-permute-start.3 = (bf16[104,768]{1,0:T(8,128)(2,1)S(1)}, bf16[104,768]{1,0:T(8,128)(2,1)S(1)}, u32[]{:S(2)}, u32[]{:S(2)}) collective-permute-start(bf16[104,768]{1,0:T(8,128)(2,1)S(1)} %pad_maximum_fusion.5), channel_id=1, source_target_pairs={{128,0},{144,16},{160,32},{176,48},{192,64},{208,80},{224,96},{240... | collective-permute-start | bytes 479240 | tf_op jit(solution)/shard_map/ppermute | solution.py:10
  516.7 26.1 %copy-start.7 = (bf16[768,768]{1,0:T(8,128)(2,1)S(1)}, bf16[768,768]{1,0:T(8,128)(2,1)}, u32[]{:S(2)}) copy-start(bf16[768,768]{1,0:T(8,128)(2,1)} %all-gather.31.cloned.1.call-done) | copy-start | bytes 3538948
  519.1 126.4 %all-gather.35.cloned.1.call-start = ((), (), s32[]{:S(2)}) async-start(), calls=%async_computation.11 | async-start | bytes 1462272 | tf_op jit(solution)/shard_map/all_gather | solution.py:28
  567.0 29.9 %copy-start.6 = (bf16[2,768,768]{2,1,0:T(8,128)(2,1)S(1)}, bf16[2,768,768]{2,1,0:T(8,128)(2,1)}, u32[]{:S(2)}) copy-start(bf16[2,768,768]{2,1,0:T(8,128)(2,1)} %all-gather.15.cloned.1.call-done) | copy-start | bytes 7077892
  569.4 4.0 collective-permute-start.4
  598.3 47.2 %copy-start.13 = (f32[2,48,768]{2,1,0:T(8,128)S(1)}, f32[2,48,768]{2,1,0:T(8,128)}, u32[]{:S(2)}) copy-start(f32[2,48,768]{2,1,0:T(8,128)} %copy-done.12) | copy-start | bytes 884740
  (4 other events, 6.7 us)
Sparse Core Ops, SparseCore 0:
  10.4 53.4 all-gather.12
  67.0 50.0 all-gather.14
  119.6 47.3 all-gather.16
  169.3 47.5 all-gather.18
  219.4 47.5 all-gather.20
  269.2 47.5 all-gather.22
  319.3 47.5 all-gather.24
  369.3 47.5 all-gather.26
  419.3 47.5 all-gather.28
  469.1 47.5 all-gather.30
  519.2 47.7 all-gather.32
  598.3 47.0 all-gather.34
where the time goes:
time: 656 us; the launch traced here: 655 us
  waiting for transfers between devices  521 us (79%)
  blocking collectives  68.9 us (11%)
  matrix products  35.2 us (5%)
  between operations  14.6 us (2%)
  starting transfers between devices  9.3 us (1%)
    all_gather x6, waiting for transfers between devices, congruence(): right_full = lax.all_gather(right_rows, 'tile', axis=0, tiled=True)  227 us
    all_gather x4, waiting for transfers between devices, on_device(): lax.all_gather(main.astype(jnp.bfloat16), 'tile', axis=0, tiled=True)  185 us
    all_gather x1, waiting for transfers between devices, on_device(): shard_rows = lax.all_gather(inverse_diag, 'tile', axis=1, tiled=True)  55.9 us
    all_gather x1, waiting for transfers between devices, on_device(): lax.all_gather(coupling_rows, 'tile', axis=1, tiled=True)  49.5 us
    all_gather x1, blocking collectives, on_device(): lax.all_gather(arrow_map_rows, 'tile', axis=1, tiled=True)  23.5 us
    all_gather x1, blocking collectives, on_device(): arrow_gathered = lax.all_gather(state_arrow, 'tile', axis=0, tiled=True)  23.2 us
    all_gather x1, blocking collectives, on_device(): arrow_whole = lax.all_gather(arrow_state, 'tile', axis=0, tiled=True)  22.2 us
    dot_general x17, matrix products, plain_dot(): return jnp.dot(left_part, right_part, preferred_element_type=jnp.float32)  18.8 us
  transfers between devices with their start and end apart: 17, of which 13 were waited for; matrix products, arithmetic and copies ran while one was open for 3% of the time, Pallas kernels for 0%

commit v1 on v0

v1 whole, which is shorter than its diff:
```python
import functools
import jax
import jax.numpy as jnp
from jax import lax
from jax.experimental import pallas as pl
from jax.experimental.pallas import tpu as pltpu
from jax.sharding import PartitionSpec as P

MESH = pl.DeviceIdType.MESH
BF, F32 = jnp.bfloat16, jnp.float32
SIDE = 4
ODD, PAIR, PLANE, TRIPLE, EVEN, SCAN1, SCAN2, SCAN3 = range(8)
OFFSETS = [(dy, dx) for dy in range(SIDE) for dx in range(SIDE) if dy or dx]
OFFSETS.sort(key=lambda o: min(o[0], 4 - o[0]) + min(o[1], 4 - o[1]))
RING = (1, 3, 2)


def tdot(a, b):
    return lax.dot_general(a, b, (((0,), (0,)), ((), ())), preferred_element_type=F32)


def dot(a, b):
    return jnp.dot(a, b, preferred_element_type=F32)


def kernel(
    planes, sizes,
    l_ref, b_ref, a_ref, z_ref, diag_ref, arrow_ref,
    full_l, full_b, full_a, wide, odd_map, odd_diag, cols, rows, tile, q_tile, m_tile,
    far_map, far_diag, part_out, part_in, part_own, q_send,
    last_m, last_q, m_row, m_col, m_total, x_send, x_in, weight, out_send, out_in, sigma,
    send_sem, recv_sem, l_send, l_recv,
):
    row, node, panel, own_arrow = sizes
    arrow = own_arrow * SIDE
    chain = lax.axis_index("chain")
    t = lax.axis_index("tile")
    z, core = chain // 2, chain % 2
    y, x = t // SIDE, t % SIDE
    widths = [min(node, -(-panel * (i + 1) // 128) * 128) for i in range(SIDE)]

    def dev(dz=0, dcore=0, dy=0, dx=0):
        zz = lax.rem(z + dz + planes, planes)
        cc = lax.rem(core + dcore, 2)
        return (zz * 2 + cc, lax.rem(y + dy + SIDE, SIDE) * SIDE + lax.rem(x + dx + SIDE, SIDE))

    used = [0]

    def take(n):
        used[0] += n
        assert used[0] <= send_sem.shape[0]
        return used[0] - n

    def copy(src, dst, sem, where):
        return pltpu.make_async_remote_copy(
            src_ref=src, dst_ref=dst, send_sem=send_sem.at[sem], recv_sem=recv_sem.at[sem],
            device_id=where, device_id_type=MESH)

    class Gather:
        def __init__(self, buf, along_x):
            self.buf, self.along_x, self.base = buf, along_x, take(3)

        def each(self, arriving):
            me = x if self.along_x else y
            for n, d in enumerate(RING):
                where = dev(dx=d) if self.along_x else dev(dy=d)
                to = lax.rem(me + SIDE - d, SIDE) if arriving else me
                yield copy(self.buf(me), self.buf(to), self.base + n, where)

        def start(self):
            for c in self.each(False):
                c.start()

        def wait(self):
            for c in self.each(True):
                c.wait_recv()
            for c in self.each(False):
                c.wait_send()

    peers = [dev(dy=dy, dx=dx) for dy, dx in OFFSETS] + [dev(dcore=1)]
    peers += [dev(dz=d) for d in (1, -1, 2, -2, 4)] + [dev(dz=1, dcore=1), dev(dz=-1, dcore=1)]
    barrier = pltpu.get_barrier_semaphore()
    for peer in peers:
        pl.semaphore_signal(barrier, inc=1, device_id=peer, device_id_type=MESH)

    my_rows = pl.ds(pl.multiple_of(t * row, 16), row)
    panel_rows = pl.ds(pl.multiple_of(x * row, 16), row)
    for b in range(2):
        for i in range(SIDE - 1):
            if widths[i] < node:
                full_l[b, panel * i:panel * (i + 1), widths[i]:] = jnp.zeros((panel, node - widths[i]), BF)
        full_l[b, my_rows, :] = l_ref[b]
        full_b[b, panel_rows, :] = b_ref[b]
    full_a[x] = jnp.concatenate([a_ref[0].astype(F32), a_ref[1].astype(F32)], axis=0).astype(BF)
    sigma[...] = tdot(z_ref[...], z_ref[...])
    pl.semaphore_wait(barrier, len(peers))

    def l_copy(b, n, w):
        dy, dx = OFFSETS[n]
        return pltpu.make_async_remote_copy(
            src_ref=l_ref.at[b, :, :w], dst_ref=full_l.at[b, my_rows, :w],
            send_sem=l_send.at[b, n], recv_sem=l_recv.at[b, t], device_id=dev(dy=dy, dx=dx), device_id_type=MESH)

    def l_each(b, do):
        for i in range(SIDE):
            @pl.when(y == i)
            def _():
                for n in range(len(OFFSETS)):
                    do(l_copy(b, n, widths[i]))

    def l_wait(b):
        for s in range(SIDE * SIDE):
            @pl.when(t != s)
            def _():
                w = widths[s // SIDE]
                pltpu.make_async_remote_copy(
                    src_ref=l_ref.at[b, :, :w], dst_ref=full_l.at[b, pl.ds(s * row, row), :w],
                    send_sem=l_send.at[b, 0], recv_sem=l_recv.at[b, s], device_id=dev(dx=1), device_id_type=MESH,
                ).wait_recv()

    def part_rows(i):
        return pl.ds(pl.multiple_of(i * row, 16), row)

    l_each(0, lambda c: c.start())
    get_b = []
    for b in range(2):
        g = Gather(lambda i, b=b: full_b.at[b, part_rows(i)], True)
        g.start()
        get_b.append(g)
        if b == 0:
            get_a = Gather(lambda i: full_a.at[i], True)
            get_a.start()
            l_each(1, lambda c: c.start())

    def block_map(b, slot):
        for j in range(0, node, 256):
            wide[:panel, j:j + 256] = -dot(full_b[b, :, j:], full_l[b, j:, j:j + 256])
            arrows = -dot(full_a[...].reshape(SIDE * 2 * own_arrow, node)[:, j:], full_l[b, j:, j:j + 256])
            for i in range(SIDE):
                lo = 2 * own_arrow * i + own_arrow * b
                wide[panel + own_arrow * i:panel + own_arrow * (i + 1), j:j + 256] = arrows[lo:lo + own_arrow]
        for c in range(SIDE):
            piece = wide[:, panel * c:panel * (c + 1)]
            rows[slot, c] = piece[:panel].astype(BF)
            if slot == ODD:
                odd_map[c] = piece.astype(BF)

            @pl.when(x == c)
            def _():
                cols[slot, y] = piece[:panel].astype(BF)
                m_tile[slot] = piece[panel:]

    def block_diag(b, slot):
        for i in range(SIDE):
            @pl.when(y == i)
            def _():
                lo = panel * i
                wide[:panel] = tdot(full_l[b, lo:, lo:lo + panel], full_l[b, lo:, :])
        for c in range(SIDE):
            piece = wide[:panel, panel * c:panel * (c + 1)]
            if slot == ODD:
                odd_diag[c] = piece.astype(BF)

            @pl.when(x == c)
            def _():
                q_tile[slot] = piece

    def get_cols(slot):
        return Gather(lambda i: cols.at[slot, i], False)

    def get_rows(slot):
        return Gather(lambda i: rows.at[slot, i], True)

    def product(left, slot):
        total = dot(left(0), cols[slot, 0])
        for k in range(1, SIDE):
            total += dot(left(k), cols[slot, k])
        return total

    def new_map(left, near, to, spread=True):
        total = product(left, near)
        arrows = total[panel:] + m_tile[near]
        m_tile[to] = arrows
        tile[to, :panel] = total[:panel].astype(BF)
        tile[to, panel:] = arrows.astype(BF)
        if spread:
            cols[to, y] = total[:panel].astype(BF)
            rows[to, x] = total[:panel].astype(BF)

    class Congruence:
        def __init__(self, index):
            self.index, self.base = index, take(3)

        def each(self, arriving):
            for n, d in enumerate(RING):
                to = lax.rem(y + d, SIDE)
                at = lax.rem(y + SIDE - d, SIDE) if arriving else y
                yield copy(part_out.at[self.index, to], part_in.at[self.index, at], self.base + n, dev(dy=d))

        def start(self, left, near):
            right = product(left, near).astype(BF)
            for s in range(SIDE):
                piece = tdot(rows[near, s], right)
                part_out[self.index, s] = piece.astype(BF)

                @pl.when(y == s)
                def _():
                    part_own[...] = piece
            for c in self.each(False):
                c.start()
            self.own = part_own[...] + q_tile[near]

        def finish(self, to):
            for c in self.each(True):
                c.wait_recv()
            total = self.own
            for d in RING:
                total += part_in[self.index, lax.rem(y + d, SIDE)].astype(F32)
            q_tile[to] = total
            q_send[to] = total.astype(BF)
            for c in self.each(False):
                c.wait_send()

    l_wait(0)
    get_b[0].wait()
    get_a.wait()
    block_map(0, EVEN)
    even_cols = get_cols(EVEN)
    even_cols.start()
    block_diag(0, EVEN)
    l_wait(1)
    get_b[1].wait()
    block_map(1, ODD)
    odd_cols = get_cols(ODD)
    odd_cols.start()
    block_diag(1, ODD)
    even_cols.wait()
    new_map(lambda k: odd_map[k], EVEN, PAIR)
    pair_cols, pair_rows = get_cols(PAIR), get_rows(PAIR)
    pair_cols.start()
    pair_rows.start()
    sibling = take(2)

    def sibling_copy(n):
        if n:
            return copy(q_send.at[PAIR], far_diag.at[0, x], sibling + 1, dev(dcore=1))
        return copy(tile.at[PAIR], far_map.at[0, x], sibling, dev(dcore=1))

    @pl.when(core == 1)
    def _():
        sibling_copy(0).start()

    pair = Congruence(0)
    pair.start(lambda k: odd_diag[k], EVEN)
    pair.finish(PAIR)

    @pl.when(core == 1)
    def _():
        sibling_copy(1).start()

    odd_cols.wait()
    pair_cols.wait()
    pair_rows.wait()

    shifts = (1, 2, 4)
    slots = (PLANE, SCAN1, SCAN2, SCAN3)
    z_base = take(8)

    def z_copy(n, diag):
        src = q_send.at[slots[n]] if diag else tile.at[slots[n]]
        dst = far_diag.at[n + 1, x] if diag else far_map.at[n + 1, x]
        return copy(src, dst, z_base + 2 * n + diag, dev(dz=-shifts[n]))

    last_base = take(4)

    def last_copy(to_core, diag):
        src = q_send.at[SCAN3] if diag else tile.at[SCAN3, pl.ds(panel, arrow)]
        dst = last_q.at[x] if diag else last_m.at[x]
        return copy(src, dst, last_base + 2 * to_core + diag, dev(dz=-1, dcore=to_core))

    far_maps = [Gather(lambda i, n=n: far_map.at[n, i], True) for n in range(4)]
    far_diags = [Gather(lambda i, n=n: far_diag.at[n, i], True) for n in range(4)]
    triple_cols, triple_rows = get_cols(TRIPLE), get_rows(TRIPLE)
    scan_cols = [get_cols(s) for s in slots[:3]]
    scan_rows = [get_rows(s) for s in slots[:3]]
    triple = Congruence(1)
    scans = [Congruence(2 + n) for n in range(4)]

    @pl.when(core == 0)
    def _():
        sibling_copy(0).wait_recv()
        far_maps[0].start()
        sibling_copy(1).wait_recv()
        far_diags[0].start()
        far_maps[0].wait()
        new_map(lambda k: far_map[0, k], PAIR, PLANE)
        scan_cols[0].start()
        scan_rows[0].start()

        @pl.when(z >= 1)
        def _():
            z_copy(0, 0).start()

        new_map(lambda k: far_map[0, k], ODD, TRIPLE)
        far_diags[0].wait()
        scans[0].start(lambda k: far_diag[0, k], PAIR)
        triple_cols.start()
        triple_rows.start()
        triple.start(lambda k: far_diag[0, k], ODD)

        @pl.when(z < planes - 1)
        def _():
            z_copy(0, 0).wait_recv()
            far_maps[1].start()

        scans[0].finish(PLANE)

        @pl.when(z >= 1)
        def _():
            z_copy(0, 1).start()

        triple.finish(TRIPLE)
        triple_cols.wait()
        triple_rows.wait()
        scan_cols[0].wait()
        scan_rows[0].wait()
        for n in range(3):
            near, to, shift = slots[n], slots[n + 1], shifts[n]

            def send_map():
                if n < 2:
                    @pl.when(z >= shifts[n + 1])
                    def _():
                        z_copy(n + 1, 0).start()
                else:
                    @pl.when(z >= 1)
                    def _():
                        last_copy(0, 0).start()
                        last_copy(1, 0).start()

            def send_diag():
                if n < 2:
                    @pl.when(z >= shifts[n + 1])
                    def _():
                        z_copy(n + 1, 1).start()
                else:
                    @pl.when(z >= 1)
                    def _():
                        last_copy(0, 1).start()
                        last_copy(1, 1).start()

            @pl.when(z + shift < planes)
            def _():
                far_maps[n + 1].wait()
                new_map(lambda k: far_map[n + 1, k], near, to, n < 2)
                send_map()
                if n < 2:
                    @pl.when(z + shifts[n + 1] < planes)
                    def _():
                        scan_cols[n + 1].start()
                        scan_rows[n + 1].start()
                z_copy(n, 1).wait_recv()
                far_diags[n + 1].start()
                far_diags[n + 1].wait()
                scans[n + 1].start(lambda k: far_diag[n + 1, k], near)
                if n < 2:
                    @pl.when(z + shifts[n + 1] < planes)
                    def _():
                        z_copy(n + 1, 0).wait_recv()
                        far_maps[n + 2].start()
                scans[n + 1].finish(to)
                send_diag()
                if n < 2:
                    @pl.when(z + shifts[n + 1] < planes)
                    def _():
                        scan_cols[n + 1].wait()
                        scan_rows[n + 1].wait()

            @pl.when(z + shift >= planes)
            def _():
                tile[to] = tile[near]
                m_tile[to] = m_tile[near]
                q_send[to] = q_send[near]
                send_map()
                send_diag()

        for n in range(3):
            @pl.when(z >= shifts[n])
            def _():
                z_copy(n, 0).wait_send()
                z_copy(n, 1).wait_send()

        @pl.when(z >= 1)
        def _():
            for k in range(2):
                last_copy(k, 0).wait_send()
                last_copy(k, 1).wait_send()

    @pl.when(core == 1)
    def _():
        sibling_copy(0).wait_send()
        sibling_copy(1).wait_send()

    finals = (jnp.where(core == 0, PLANE, PAIR), jnp.where(core == 0, TRIPLE, ODD))
    get_m = Gather(lambda i: last_m.at[i], True)
    get_q = Gather(lambda i: last_q.at[i], True)

    def last_wait(diag):
        for k in range(2):
            @pl.when(core == k)
            def _():
                last_copy(k, diag).wait_recv()

    @pl.when(z < planes - 1)
    def _():
        last_wait(0)
        get_m.start()
        get_m.wait()

    get_mr, get_mc = [], []
    for j in range(2):
        @pl.when(z < planes - 1)
        def _():
            m_total[j] = product(lambda k: last_m[k], finals[j]) + m_tile[finals[j]]

        @pl.when(z == planes - 1)
        def _():
            m_total[j] = m_tile[finals[j]]

        m_row[j, x] = m_total[j].astype(BF)
        m_col[j, y] = m_total[j].astype(BF)
        get_mr.append(Gather(lambda i, j=j: m_row.at[j, i], True))
        get_mc.append(Gather(lambda i, j=j: m_col.at[j, i], False))
        get_mr[j].start()
        get_mc[j].start()
    x_base = take(6)

    def x_each(j, arriving):
        for n, d in enumerate(RING):
            to = lax.rem(x + d, SIDE)
            at = lax.rem(x + SIDE - d, SIDE) if arriving else x
            src = x_send.at[j, pl.ds(pl.multiple_of(to * own_arrow, 8), own_arrow)]
            yield copy(src, x_in.at[j, at], x_base + 3 * j + n, dev(dx=d))

    sigma_rows = sigma[pl.ds(pl.multiple_of(y * arrow, 8), arrow)]
    for j in range(2):
        get_mr[j].wait()
        get_mc[j].wait()
        x_send[j] = lax.dot_general(
            sigma_rows, m_col[j].reshape(SIDE * arrow, panel).astype(F32), (((1,), (0,)), ((), ())),
            precision=lax.Precision.HIGHEST, preferred_element_type=F32)
        x_in[j, x] = x_send[j, pl.ds(pl.multiple_of(x * own_arrow, 8), own_arrow)]
        for c in x_each(j, False):
            c.start()

    @pl.when(z < planes - 1)
    def _():
        last_wait(1)
        get_q.start()
        get_q.wait()
        for j in range(2):
            weight[j] = product(lambda k: last_q[k], finals[j]).astype(BF)

    @pl.when(z == planes - 1)
    def _():
        weight[...] = jnp.zeros_like(weight)

    out_base = take(2 * len(OFFSETS))

    def out_each(j, arriving):
        for n, (dy, dx) in enumerate(OFFSETS):
            ty, tx = lax.rem(y + dy, SIDE), lax.rem(x + dx, SIDE)
            at = (lax.rem(y + SIDE - dy, SIDE), lax.rem(x + SIDE - dx, SIDE)) if arriving else (y, x)
            src = out_send.at[j, ty, pl.ds(pl.multiple_of(tx * row, 16), row)]
            yield copy(src, out_in.at[j, at[0], at[1]], out_base + len(OFFSETS) * j + n, dev(dy=dy, dx=dx))

    for j in range(2):
        arrows = x_send[j].astype(BF)
        for s in range(SIDE):
            part_own[...] = tdot(rows[finals[j], s], weight[j]) + tdot(m_row[j, s], arrows)

            @pl.when(y == s)
            def _():
                part_own[...] += q_tile[finals[j]]
            out_send[j, s] = part_own[...].astype(BF)
        out_in[j, y, x] = out_send[j, y, pl.ds(pl.multiple_of(x * row, 16), row)]
        for c in out_each(j, False):
            c.start()
    for j in range(2):
        for c in x_each(j, True):
            c.wait_recv()
        for i in range(SIDE):
            arrow_ref[j, :, panel * i:panel * (i + 1)] = x_in[j, i]
        for c in x_each(j, False):
            c.wait_send()
    for j in range(2):
        for c in out_each(j, True):
            c.wait_recv()
        for i in range(SIDE):
            total = out_in[j, 0, i].astype(F32)
            for k in range(1, SIDE):
                total += out_in[j, k, i].astype(F32)
            diag_ref[j, :, panel * i:panel * (i + 1)] = total
    for j in range(2):
        for c in out_each(j, False):
            c.wait_send()
    for b in range(2):
        l_each(b, lambda c: c.wait_send())


def solution(mesh):
    planes = mesh.shape["chain"] // 2

    def on_device(inverse_diag, sub_diag, arrow_rows, arrow_inverse):
        count, row, node = inverse_diag.shape
        own_arrow = arrow_rows.shape[1]
        panel, arrow = row * SIDE, own_arrow * SIDE
        vm = pltpu.VMEM
        scratch = [
            vm((2, node, node), BF), vm((2, panel, node), BF), vm((SIDE, 2 * own_arrow, node), BF),
            vm((panel + arrow, node), F32),
            vm((SIDE, panel + arrow, panel), BF), vm((SIDE, panel, panel), BF),
            vm((7, SIDE, panel, panel), BF), vm((7, SIDE, panel, panel), BF),
            vm((8, panel + arrow, panel), BF), vm((8, panel, panel), F32), vm((8, arrow, panel), F32),
            vm((4, SIDE, panel + arrow, panel), BF), vm((4, SIDE, panel, panel), BF),
            vm((6, SIDE, panel, panel), BF), vm((6, SIDE, panel, panel), BF), vm((panel, panel), F32),
            vm((8, panel, panel), BF),
            vm((SIDE, arrow, panel), BF), vm((SIDE, panel, panel), BF),
            vm((2, SIDE, arrow, panel), BF), vm((2, SIDE, arrow, panel), BF), vm((2, arrow, panel), F32),
            vm((2, arrow, panel), F32), vm((2, SIDE, own_arrow, panel), F32),
            vm((2, panel, panel), BF), vm((2, SIDE, panel, panel), BF), vm((2, SIDE, SIDE, row, panel), BF),
            vm(arrow_inverse.shape, F32),
            pltpu.SemaphoreType.DMA((160,)), pltpu.SemaphoreType.DMA((160,)),
            pltpu.SemaphoreType.DMA((2, 15)), pltpu.SemaphoreType.DMA((2, 16)),
        ]
        return pl.pallas_call(
            functools.partial(kernel, planes, (row, node, panel, own_arrow)),
            out_shape=(
                jax.ShapeDtypeStruct(inverse_diag.shape, F32),
                jax.ShapeDtypeStruct(arrow_rows.shape, F32),
            ),
            in_specs=[pl.BlockSpec(memory_space=vm)] * 4,
            out_specs=(pl.BlockSpec(memory_space=vm),) * 2,
            scratch_shapes=scratch,
            compiler_params=pltpu.CompilerParams(
                collective_id=0, has_side_effects=True, vmem_limit_bytes=52 << 20),
            name="selected_inverse",
        )(inverse_diag, sub_diag, arrow_rows, arrow_inverse)

    placed = P("chain", "tile", None)
    return jax.shard_map(
        on_device, mesh=mesh, in_specs=(placed, placed, placed, P()), out_specs=(placed, placed), check_vma=False)
```

time: 656 us -> 163 us (0.25)
  waiting for transfers between devices: 521 us -> 0 us
  Pallas kernels: 0 us -> 155 us
  blocking collectives: 68.9 us -> 0 us
  matrix products: 35.2 us -> 0 us
  between operations: 14.6 us -> 0.65 us
  starting transfers between devices: 9.3 us -> 0 us
    all_gather x12 -> x0, waiting for transfers between devices: 518 us -> none  [the longest x6 227 us: congruence(): right_full = lax.all_gather(right_rows, 'tile', axis=0, tiled=True)]
    pallas_call x0 -> x1, Pallas kernels: none -> 155 us  [on_device(): pl.pallas_call(functools.partial(kernel, planes, (row, node, panel, own_a...]
    all_gather x3 -> x0, blocking collectives: 68.9 us -> none  [the longest x1 23.5 us: on_device(): lax.all_gather(arrow_map_rows, 'tile', axis=1, tiled=True)]
    dot_general x30 -> x0, matrix products: 35.2 us -> none  [the longest x17 18.8 us: plain_dot(): return jnp.dot(left_part, right_part, preferred_element_type=jnp.float32)]
    ppermute x5 -> x0, starting transfers between devices: 8.81 us -> none  [shifted(): lax.ppermute(value, axis, [(source, source + steps) for source in range(f...]
  transfers between devices with their start and end apart: 17 -> 0, of which waited for: 13 -> 0; matrix products, arithmetic and copies ran while one was open for 3% -> 0% of each run, Pallas kernels for 0% -> 0%
where the time goes in v1:
time: 163 us; the launch traced here: 160 us
  Pallas kernels  155 us (95%)
  local copies, waits for them, and re-layouts  4.64 us (3%)
    pallas_call x1, Pallas kernels, on_device(): pl.pallas_call(functools.partial(kernel, planes, (row, node, panel, own_a...  155 us
    unnamed x10, local copies, waits for them, and re-layouts  4.64 us

profile of v1, /device:TPU:32, one launch (start us, length us, event | category | flops | bytes accessed | tf_op | source)
XLA Modules:
  0.0 160.2 jit_solution(5547574559918698319)
XLA Ops:
  0.6 0.0 copy-start
  0.6 0.9 copy-done
  1.5 0.0 copy-start.1
  1.5 0.9 copy-done.1
  2.5 0.0 copy-start.2
  2.5 0.8 copy-done.2
  3.2 0.0 copy-start.3
  3.2 0.7 copy-done.3
  3.9 154.9 %selected_inverse.1 = (f32[2,48,768]{2,1,0:T(8,128)S(1)}, f32[2,8,768]{2,1,0:T(8,128)S(1)}) custom-call(bf16[2,48,768]{2,1,0:T(8,128)(2,1)S(1)} %copy-done, bf16[2,48,768]{2,1,0:T(8,128)(2,1)S(1)} %copy-done.1, bf16[2,8,768]{2,1,0:T(8,128)(2,1)S(1)} %copy-done.3, bf16[128,128]{1,0:T(8,128)(2,1)S(1)} %copy-done.2), custom_call_target="tpu_custom_call" | custom-call | tf_op jit(solution)/shard_map/selected_inverse/pallas_call | solution.py:536
  158.9 0.7 copy.8
  159.6 0.6 copy.9
Async XLA Ops:
  0.6 0.9 copy-start
  1.5 0.9 copy-start.1
  2.5 0.8 copy-start.2
  3.2 0.7 copy-start.3

commit v2 on v1

v2 whole, which is shorter than its diff:
```python
import functools
import jax
import jax.numpy as jnp
from jax import lax
from jax.experimental import pallas as pl
from jax.experimental.pallas import tpu as pltpu
from jax.sharding import PartitionSpec as P

MESH = pl.DeviceIdType.MESH
BF, F32 = jnp.bfloat16, jnp.float32
SIDE = 4
ODD, PAIR, PLANE, TRIPLE, EVEN, SCAN1, SCAN2 = range(7)
LONG = 6
OFFSETS = [(dy, dx) for dy in range(SIDE) for dx in range(SIDE) if dy or dx]
OFFSETS.sort(key=lambda o: min(o[0], 4 - o[0]) + min(o[1], 4 - o[1]))
RING = (1, 3, 2)
FAN = (2, 1, 3, 0)


def tdot(a, b):
    return lax.dot_general(a, b, (((0,), (0,)), ((), ())), preferred_element_type=F32)


def dot(a, b):
    return jnp.dot(a, b, preferred_element_type=F32)


def kernel(
    planes, sizes,
    l_in, b_in, a_in, z_in, diag_ref, arrow_ref,
    l_ref, b_ref, a_ref, z_ref, full_l, full_b, full_a, both_a, wide, wide_d, arrows_all, own_tiles, even, odd_far,
    cols, rows, tile, q_tile, m_tile, far_map, far_diag, part_out, part_in, part_own, q_send,
    a_map, a_diag, b_arrow, b_diag, m_row, m_col, m_total, x_send, x_in, weight, out_send, out_in, sigma,
    send_sem, recv_sem, l_send, l_recv, load_sem,
):
    row, node, panel, own_arrow = sizes
    arrow = own_arrow * SIDE
    chain = lax.axis_index("chain")
    t = lax.axis_index("tile")
    z, core = chain // 2, chain % 2
    y, x = t // SIDE, t % SIDE
    widths = [min(node, -(-panel * (i + 1) // 128) * 128) for i in range(SIDE)]
    loads = [pltpu.make_async_copy(src, dst, load_sem.at[n]) for n, (src, dst) in enumerate(
        ((l_in, l_ref), (b_in, b_ref), (a_in, a_ref), (z_in, z_ref)))]
    for load in loads:
        load.start()

    def dev(dz=0, dcore=0, dy=0, dx=0):
        zz = lax.rem(z + dz + planes, planes)
        cc = lax.rem(core + dcore, 2)
        return (zz * 2 + cc, lax.rem(y + dy + SIDE, SIDE) * SIDE + lax.rem(x + dx + SIDE, SIDE))

    used = [0]

    def take(n):
        used[0] += n
        assert used[0] <= send_sem.shape[0]
        return used[0] - n

    def copy(src, dst, sem, where):
        return pltpu.make_async_remote_copy(
            src_ref=src, dst_ref=dst, send_sem=send_sem.at[sem], recv_sem=recv_sem.at[sem],
            device_id=where, device_id_type=MESH)

    class Gather:
        def __init__(self, buf, along_x):
            self.buf, self.along_x, self.base = buf, along_x, take(3)

        def each(self, arriving):
            me = x if self.along_x else y
            for n, d in enumerate(RING):
                where = dev(dx=d) if self.along_x else dev(dy=d)
                to = lax.rem(me + SIDE - d, SIDE) if arriving else me
                yield copy(self.buf(me), self.buf(to), self.base + n, where)

        def start(self):
            for c in self.each(False):
                c.start()

        def wait(self):
            for c in self.each(True):
                c.wait_recv()
            for c in self.each(False):
                c.wait_send()

    barrier = pltpu.get_barrier_semaphore()
    group = [dev(dy=dy, dx=dx) for dy, dx in OFFSETS]
    first = [dev(dcore=1, dx=d) for d in range(SIDE)] + [dev(dz=d) for d in (1, 2, -3)]
    second = [dev(dz=d, dcore=1) for d in (1, -3)]
    for peer in group:
        pl.semaphore_signal(barrier, inc=1, device_id=peer, device_id_type=MESH)
    for k, others in enumerate((first, second)):
        @pl.when(core == k)
        def _():
            for peer in others:
                pl.semaphore_signal(barrier, inc=1, device_id=peer, device_id_type=MESH)

    my_rows = pl.ds(pl.multiple_of(t * row, 16), row)
    panel_rows = pl.ds(pl.multiple_of(x * row, 16), row)
    mine = x // 2 == core
    block = lax.rem(x, 2)
    for i in range(SIDE - 1):
        if widths[i] < node:
            full_l[panel * i:panel * (i + 1), widths[i]:] = jnp.zeros((panel, node - widths[i]), BF)
    for load in loads:
        load.wait()
    both_a[...] = jnp.concatenate([a_ref[0].astype(F32), a_ref[1].astype(F32)], axis=0).astype(BF)
    for k, extra in enumerate((5, SIDE)):
        @pl.when(core == k)
        def _():
            pl.semaphore_wait(barrier, len(group) + extra)

    def to_column(b, dy):
        owner = 2 * core + b
        return (chain, lax.rem(y + dy, SIDE) * SIDE + owner)

    def l_copy(b, dy, w):
        return pltpu.make_async_remote_copy(
            src_ref=l_ref.at[b, :, :w], dst_ref=full_l.at[my_rows, :w], send_sem=l_send.at[b, dy],
            recv_sem=l_recv.at[t], device_id=to_column(b, dy), device_id_type=MESH)

    def b_copy(b):
        return pltpu.make_async_remote_copy(
            src_ref=b_ref.at[b], dst_ref=full_b.at[panel_rows], send_sem=l_send.at[b, 4],
            recv_sem=l_recv.at[16 + x], device_id=to_column(b, 0), device_id_type=MESH)

    def a_copy(b):
        return pltpu.make_async_remote_copy(
            src_ref=both_a, dst_ref=full_a.at[x], send_sem=l_send.at[b, 5],
            recv_sem=l_recv.at[20 + x], device_id=to_column(b, 0), device_id_type=MESH)

    def spread(do):
        for b in range(2):
            for i in range(SIDE):
                @pl.when(y == i)
                def _():
                    for dy in (1, 3, 2):
                        do(l_copy(b, dy, widths[i]))

            @pl.when(x != 2 * core + b)
            def _():
                for i in range(SIDE):
                    @pl.when(y == i)
                    def _():
                        do(l_copy(b, 0, widths[i]))
                do(b_copy(b))
                do(a_copy(b))

    spread(lambda c: c.start())
    sigma[...] = tdot(z_ref[...], z_ref[...])
    tile_base = take(3)

    def tile_send(b, n):
        to = lax.rem(x + RING[n], SIDE)
        dst = odd_far.at[to] if b else even
        return pltpu.make_async_remote_copy(
            src_ref=own_tiles.at[to], dst_ref=dst, send_sem=send_sem.at[tile_base + n],
            recv_sem=l_recv.at[24 + b], device_id=dev(dx=RING[n]), device_id_type=MESH)

    @pl.when(mine)
    def _():
        for b in range(2):
            @pl.when(block == b)
            def _():
                full_l[my_rows, :] = l_ref[b]
                full_b[panel_rows, :] = b_ref[b]
        full_a[x] = both_a[...]
        for s in range(SIDE * SIDE):
            @pl.when(t != s)
            def _():
                w = widths[s // SIDE]
                pltpu.make_async_remote_copy(
                    src_ref=l_ref.at[0, :, :w], dst_ref=full_l.at[pl.ds(s * row, row), :w],
                    send_sem=l_send.at[0, 0], recv_sem=l_recv.at[s], device_id=dev(dx=1), device_id_type=MESH,
                ).wait_recv()
        for s in range(SIDE):
            @pl.when(x != s)
            def _():
                pltpu.make_async_remote_copy(
                    src_ref=b_ref.at[0], dst_ref=full_b.at[pl.ds(s * row, row)], send_sem=l_send.at[0, 4],
                    recv_sem=l_recv.at[16 + s], device_id=dev(dx=1), device_id_type=MESH).wait_recv()
                pltpu.make_async_remote_copy(
                    src_ref=both_a, dst_ref=full_a.at[s], send_sem=l_send.at[0, 5],
                    recv_sem=l_recv.at[20 + s], device_id=dev(dx=1), device_id_type=MESH).wait_recv()
        for j in range(0, node, 256):
            wide[:panel, j:j + 256] = -dot(full_b[:, j:], full_l[j:, j:j + 256])
            arrows_all[:, j:j + 256] = -dot(full_a[...].reshape(SIDE * 2 * own_arrow, node)[:, j:], full_l[j:, j:j + 256])
        for i in range(SIDE):
            lo = pl.multiple_of(2 * own_arrow * i + own_arrow * block, 8)
            wide[panel + own_arrow * i:panel + own_arrow * (i + 1)] = arrows_all[pl.ds(lo, own_arrow)]
        for i in range(SIDE):
            @pl.when(y == i)
            def _():
                lo = panel * i
                wide_d[...] = tdot(full_l[lo:, lo:lo + panel], full_l[lo:, :])
        for c in range(SIDE):
            own_tiles[c, :panel + arrow] = wide[:, panel * c:panel * (c + 1)].astype(BF)
            own_tiles[c, panel + arrow:] = wide_d[:, panel * c:panel * (c + 1)].astype(BF)
        for b in range(2):
            @pl.when(block == b)
            def _():
                for n in range(3):
                    tile_send(b, n).start()
                if b:
                    odd_far[x] = own_tiles[x]
                else:
                    even[...] = own_tiles[x]

    def get_cols(slot):
        return Gather(lambda i: cols.at[slot, i], False)

    def get_rows(slot):
        return Gather(lambda i: rows.at[slot, i], True)

    def product(left, slot):
        total = dot(left(0), cols[slot, 0])
        for k in range(1, SIDE):
            total += dot(left(k), cols[slot, k])
        return total

    def new_map(left, near, to, spread=True):
        total = product(left, near)
        arrows = total[panel:] + m_tile[near]
        m_tile[to] = arrows
        tile[to, :panel] = total[:panel].astype(BF)
        tile[to, panel:] = arrows.astype(BF)
        if spread:
            cols[to, y] = total[:panel].astype(BF)
            rows[to, x] = total[:panel].astype(BF)

    class Congruence:
        def __init__(self, index):
            self.index, self.base = index, take(3)

        def each(self, arriving):
            for n, d in enumerate(RING):
                to = lax.rem(y + d, SIDE)
                at = lax.rem(y + SIDE - d, SIDE) if arriving else y
                yield copy(part_out.at[self.index, to], part_in.at[self.index, at], self.base + n, dev(dy=d))

        def start(self, left, near):
            right = product(left, near).astype(BF)
            for s in range(SIDE):
                piece = tdot(rows[near, s], right)
                part_out[self.index, s] = piece.astype(BF)

                @pl.when(y == s)
                def _():
                    part_own[self.index] = piece + q_tile[near]
            for c in self.each(False):
                c.start()

        def finish(self, to):
            for c in self.each(True):
                c.wait_recv()
            total = part_own[self.index]
            for d in RING:
                total += part_in[self.index, lax.rem(y + d, SIDE)].astype(F32)
            q_tile[to] = total
            q_send[to] = total.astype(BF)
            for c in self.each(False):
                c.wait_send()

    for b in (1, 0):
        @pl.when(x != 2 * core + b)
        def _():
            pltpu.make_async_remote_copy(
                src_ref=own_tiles.at[0], dst_ref=odd_far.at[x] if b else even, send_sem=send_sem.at[tile_base],
                recv_sem=l_recv.at[24 + b], device_id=dev(dx=1), device_id_type=MESH).wait_recv()
    cols[EVEN, y] = even[:panel]
    rows[EVEN, x] = even[:panel]
    even_cols, even_rows, odd_cols = get_cols(EVEN), get_rows(EVEN), get_cols(ODD)
    odd_panel = Gather(lambda i: odd_far.at[i], True)
    even_cols.start()
    odd_panel.start()
    even_rows.start()
    cols[ODD, y] = odd_far[x, :panel]
    m_tile[EVEN] = even[panel:panel + arrow].astype(F32)
    q_tile[EVEN] = even[panel + arrow:].astype(F32)
    m_tile[ODD] = odd_far[x, panel:panel + arrow].astype(F32)
    q_tile[ODD] = odd_far[x, panel + arrow:].astype(F32)
    even_cols.wait()
    odd_panel.wait()
    new_map(lambda k: odd_far[k, :panel + arrow], EVEN, PAIR)
    fan = take(8)

    def fan_copy(d, diag):
        src = q_send.at[PAIR] if diag else tile.at[PAIR]
        dst = far_diag.at[0, x] if diag else far_map.at[0, x]
        return copy(src, dst, fan + 4 * diag + d, dev(dcore=1, dx=d))

    def fan_wait(diag):
        for d in range(SIDE):
            at = lax.rem(x + SIDE - d, SIDE)
            src = q_send.at[PAIR] if diag else tile.at[PAIR]
            dst = far_diag.at[0, at] if diag else far_map.at[0, at]
            copy(src, dst, fan + 4 * diag + d, dev(dcore=1, dx=d)).wait_recv()

    @pl.when(core == 1)
    def _():
        for d in FAN:
            fan_copy(d, 0).start()

    pair_cols, pair_rows = get_cols(PAIR), get_rows(PAIR)
    pair = Congruence(0)
    even_rows.wait()
    pair.start(lambda k: odd_far[k, panel + arrow:], EVEN)
    pair_cols.start()
    pair_rows.start()
    odd_cols.start()
    for k in range(SIDE):
        rows[ODD, k] = odd_far[k, :panel]
    pair.finish(PAIR)

    @pl.when(core == 1)
    def _():
        for d in FAN:
            fan_copy(d, 1).start()

    pair_cols.wait()
    pair_rows.wait()
    odd_cols.wait()

    shifts = (1, 2)
    slots = (PLANE, SCAN1, SCAN2)
    z_base = take(4)

    def z_copy(n, diag):
        src = q_send.at[slots[n]] if diag else tile.at[slots[n]]
        dst = far_diag.at[n + 1, x] if diag else far_map.at[n + 1, x]
        return copy(src, dst, z_base + 2 * n + diag, dev(dz=-shifts[n]))

    last_base = take(8)

    def last_copy(far, to_core, diag):
        if far:
            src = q_send.at[SCAN2] if diag else tile.at[SCAN2, pl.ds(panel, arrow)]
            dst = b_diag.at[x] if diag else b_arrow.at[x]
        else:
            src = q_send.at[SCAN2] if diag else tile.at[SCAN2]
            dst = a_diag.at[x] if diag else a_map.at[x]
        return copy(src, dst, last_base + 4 * far + 2 * to_core + diag, dev(dz=-5 if far else -1, dcore=to_core))

    def last_each(diag, do):
        for far, steps in ((0, 1), (1, 5)):
            @pl.when(z >= steps)
            def _():
                for k in range(2):
                    do(last_copy(far, k, diag))

    def last_wait(far, diag):
        for k in range(2):
            @pl.when(core == k)
            def _():
                last_copy(far, k, diag).wait_recv()

    far_maps = [None] + [Gather(lambda i, n=n: far_map.at[n, i], True) for n in (1, 2)]
    far_diags = [None] + [Gather(lambda i, n=n: far_diag.at[n, i], True) for n in (1, 2)]
    triple_cols, triple_rows = get_cols(TRIPLE), get_rows(TRIPLE)
    scan_cols = [get_cols(s) for s in slots[:2]]
    scan_rows = [get_rows(s) for s in slots[:2]]
    triple = Congruence(1)
    scans = [Congruence(2 + n) for n in range(3)]
    has_a, has_b = z + 1 < planes, z + 5 < planes
    get_am = Gather(lambda i: a_map.at[i], True)
    get_bm = Gather(lambda i: b_arrow.at[i], True)
    get_aq = Gather(lambda i: a_diag.at[i], True)
    get_bq = Gather(lambda i: b_diag.at[i], True)
    long_cols, long_rows = [get_cols(LONG + j) for j in range(2)], [get_rows(LONG + j) for j in range(2)]
    finals = (jnp.where(core == 0, PLANE, PAIR), jnp.where(core == 0, TRIPLE, ODD))

    @pl.when(core == 0)
    def _():
        fan_wait(0)
        new_map(lambda k: far_map[0, k], PAIR, PLANE)

        @pl.when(z >= 1)
        def _():
            z_copy(0, 0).start()

        scan_cols[0].start()
        scan_rows[0].start()
        fan_wait(1)
        scans[0].start(lambda k: far_diag[0, k], PAIR)

        @pl.when(has_a)
        def _():
            z_copy(0, 0).wait_recv()
            far_maps[1].start()

        scans[0].finish(PLANE)

        @pl.when(z >= 1)
        def _():
            z_copy(0, 1).start()

        new_map(lambda k: far_map[0, k], ODD, TRIPLE)
        triple.start(lambda k: far_diag[0, k], ODD)
        scan_cols[0].wait()
        scan_rows[0].wait()

        @pl.when(has_a)
        def _():
            far_maps[1].wait()
            new_map(lambda k: far_map[1, k], PLANE, SCAN1)

            @pl.when(z >= 2)
            def _():
                z_copy(1, 0).start()

            @pl.when(z + 2 < planes)
            def _():
                scan_cols[1].start()
                scan_rows[1].start()
            z_copy(0, 1).wait_recv()
            far_diags[1].start()
            far_diags[1].wait()
            scans[1].start(lambda k: far_diag[1, k], PLANE)

            @pl.when(z + 2 < planes)
            def _():
                z_copy(1, 0).wait_recv()
                far_maps[2].start()
            scans[1].finish(SCAN1)

        @pl.when(z + 1 == planes)
        def _():
            tile[SCAN1] = tile[PLANE]
            m_tile[SCAN1] = m_tile[PLANE]
            q_send[SCAN1] = q_send[PLANE]
            z_copy(1, 0).start()

        @pl.when(z >= 2)
        def _():
            z_copy(1, 1).start()

        triple_cols.start()
        triple_rows.start()
        triple.finish(TRIPLE)

        @pl.when(z + 2 < planes)
        def _():
            scan_cols[1].wait()
            scan_rows[1].wait()
            far_maps[2].wait()
            new_map(lambda k: far_map[2, k], SCAN1, SCAN2, False)

        @pl.when(z + 2 >= planes)
        def _():
            tile[SCAN2] = tile[SCAN1]
            q_send[SCAN2] = q_send[SCAN1]

        last_each(0, lambda c: c.start())

        @pl.when(z + 2 >= planes)
        def _():
            last_each(1, lambda c: c.start())

        triple_cols.wait()
        triple_rows.wait()

        @pl.when(z + 2 < planes)
        def _():
            z_copy(1, 1).wait_recv()
            far_diags[2].start()

    @pl.when(has_a)
    def _():
        last_wait(0, 0)
        get_am.start()

    @pl.when(has_b)
    def _():
        last_wait(1, 0)
        get_bm.start()

    @pl.when((core == 0) & (z + 2 < planes))
    def _():
        far_diags[2].wait()
        scans[2].start(lambda k: far_diag[2, k], SCAN1)

    @pl.when(has_a)
    def _():
        get_am.wait()
        for j in range(2):
            total = product(lambda k: a_map[k], finals[j])
            m_total[j] = total[panel:] + m_tile[finals[j]]

            @pl.when(has_b)
            def _():
                cols[LONG + j, y] = total[:panel].astype(BF)
                rows[LONG + j, x] = total[:panel].astype(BF)
                long_cols[j].start()
                long_rows[j].start()

    @pl.when(z + 1 == planes)
    def _():
        for j in range(2):
            m_total[j] = m_tile[finals[j]]

    @pl.when((core == 0) & (z + 2 < planes))
    def _():
        scans[2].finish(SCAN2)
        last_each(1, lambda c: c.start())

    @pl.when(has_b)
    def _():
        get_bm.wait()
        for j in range(2):
            long_cols[j].wait()
            m_total[j] += product(lambda k: b_arrow[k], LONG + j)

    get_mr, get_mc = [], []
    for j in range(2):
        m_row[j, x] = m_total[j].astype(BF)
        m_col[j, y] = m_total[j].astype(BF)
        get_mr.append(Gather(lambda i, j=j: m_row.at[j, i], True))
        get_mc.append(Gather(lambda i, j=j: m_col.at[j, i], False))
        get_mr[j].start()
        get_mc[j].start()

    @pl.when(has_a)
    def _():
        last_wait(0, 1)
        get_aq.start()

    @pl.when(has_b)
    def _():
        last_wait(1, 1)
        get_bq.start()

    x_base = take(6)

    def x_each(j, arriving):
        for n, d in enumerate(RING):
            to = lax.rem(x + d, SIDE)
            at = lax.rem(x + SIDE - d, SIDE) if arriving else x
            src = x_send.at[j, pl.ds(pl.multiple_of(to * own_arrow, 8), own_arrow)]
            yield copy(src, x_in.at[j, at], x_base + 3 * j + n, dev(dx=d))

    sigma_rows = sigma[pl.ds(pl.multiple_of(y * arrow, 8), arrow)]
    for j in range(2):
        get_mr[j].wait()
        get_mc[j].wait()
        x_send[j] = lax.dot_general(
            sigma_rows, m_col[j].reshape(SIDE * arrow, panel).astype(F32), (((1,), (0,)), ((), ())),
            precision=lax.Precision.HIGHEST, preferred_element_type=F32)
        x_in[j, x] = x_send[j, pl.ds(pl.multiple_of(x * own_arrow, 8), own_arrow)]
        for c in x_each(j, False):
            c.start()

    @pl.when(has_a)
    def _():
        get_aq.wait()
        for j in range(2):
            weight[j] = product(lambda k: a_diag[k], finals[j]).astype(BF)

    @pl.when(has_b)
    def _():
        get_bq.wait()
        for j in range(2):
            long_rows[j].wait()
            weight[2 + j] = product(lambda k: b_diag[k], LONG + j).astype(BF)

    out_base = take(2 * len(OFFSETS))

    def out_each(j, arriving):
        for n, (dy, dx) in enumerate(OFFSETS):
            ty, tx = lax.rem(y + dy, SIDE), lax.rem(x + dx, SIDE)
            at = (lax.rem(y + SIDE - dy, SIDE), lax.rem(x + SIDE - dx, SIDE)) if arriving else (y, x)
            src = out_send.at[j, ty, pl.ds(pl.multiple_of(tx * row, 16), row)]
            yield copy(src, out_in.at[j, at[0], at[1]], out_base + len(OFFSETS) * j + n, dev(dy=dy, dx=dx))

    for j in range(2):
        arrows = x_send[j].astype(BF)
        for s in range(SIDE):
            part_own[5] = tdot(m_row[j, s], arrows)

            @pl.when(has_a)
            def _():
                part_own[5] += tdot(rows[finals[j], s], weight[j])

            @pl.when(has_b)
            def _():
                part_own[5] += tdot(rows[LONG + j, s], weight[2 + j])

            @pl.when(y == s)
            def _():
                part_own[5] += q_tile[finals[j]]
            out_send[j, s] = part_own[5].astype(BF)
        out_in[j, y, x] = out_send[j, y, pl.ds(pl.multiple_of(x * row, 16), row)]
        for c in out_each(j, False):
            c.start()
    for j in range(2):
        for c in x_each(j, True):
            c.wait_recv()
        for i in range(SIDE):
            arrow_ref[j, :, panel * i:panel * (i + 1)] = x_in[j, i]
        for c in x_each(j, False):
            c.wait_send()
    for j in range(2):
        for c in out_each(j, True):
            c.wait_recv()
        for i in range(SIDE):
            total = out_in[j, 0, i].astype(F32)
            for k in range(1, SIDE):
                total += out_in[j, k, i].astype(F32)
            diag_ref[j, :, panel * i:panel * (i + 1)] = total
    for j in range(2):
        for c in out_each(j, False):
            c.wait_send()
    spread(lambda c: c.wait_send())

    @pl.when(mine)
    def _():
        for n in range(3):
            tile_send(0, n).wait_send()

    @pl.when(core == 1)
    def _():
        for d in FAN:
            fan_copy(d, 0).wait_send()
            fan_copy(d, 1).wait_send()

    @pl.when(core == 0)
    def _():
        for n in range(2):
            @pl.when(z >= shifts[n])
            def _():
                z_copy(n, 0).wait_send()
                z_copy(n, 1).wait_send()
        last_each(0, lambda c: c.wait_send())
        last_each(1, lambda c: c.wait_send())


def solution(mesh):
    planes = mesh.shape["chain"] // 2

    def on_device(inverse_diag, sub_diag, arrow_rows, arrow_inverse):
        count, row, node = inverse_diag.shape
        own_arrow = arrow_rows.shape[1]
        panel, arrow = row * SIDE, own_arrow * SIDE
        vm = pltpu.VMEM
        scratch = [
            vm(inverse_diag.shape, BF), vm(sub_diag.shape, BF), vm(arrow_rows.shape, BF), vm(arrow_inverse.shape, BF),
            vm((node, node), BF), vm((panel, node), BF), vm((SIDE, 2 * own_arrow, node), BF), vm((2 * own_arrow, node), BF),
            vm((panel + arrow, node), F32), vm((panel, node), F32), vm((2 * arrow, node), F32),
            vm((SIDE, 2 * panel + arrow, panel), BF), vm((2 * panel + arrow, panel), BF),
            vm((SIDE, 2 * panel + arrow, panel), BF),
            vm((8, SIDE, panel, panel), BF), vm((8, SIDE, panel, panel), BF),
            vm((7, panel + arrow, panel), BF), vm((7, panel, panel), F32), vm((7, arrow, panel), F32),
            vm((3, SIDE, panel + arrow, panel), BF), vm((3, SIDE, panel, panel), BF),
            vm((5, SIDE, panel, panel), BF), vm((5, SIDE, panel, panel), BF), vm((6, panel, panel), F32),
            vm((7, panel, panel), BF),
            vm((SIDE, panel + arrow, panel), BF), vm((SIDE, panel, panel), BF),
            vm((SIDE, arrow, panel), BF), vm((SIDE, panel, panel), BF),
            vm((2, SIDE, arrow, panel), BF), vm((2, SIDE, arrow, panel), BF), vm((2, arrow, panel), F32),
            vm((2, arrow, panel), F32), vm((2, SIDE, own_arrow, panel), F32),
            vm((4, panel, panel), BF), vm((2, SIDE, panel, panel), BF), vm((2, SIDE, SIDE, row, panel), BF),
            vm(arrow_inverse.shape, F32),
            pltpu.SemaphoreType.DMA((200,)), pltpu.SemaphoreType.DMA((200,)),
            pltpu.SemaphoreType.DMA((2, 6)), pltpu.SemaphoreType.DMA((26,)), pltpu.SemaphoreType.DMA((4,)),
        ]
        return pl.pallas_call(
            functools.partial(kernel, planes, (row, node, panel, own_arrow)),
            out_shape=(
                jax.ShapeDtypeStruct(inverse_diag.shape, F32),
                jax.ShapeDtypeStruct(arrow_rows.shape, F32),
            ),
            in_specs=[pl.BlockSpec(memory_space=pl.ANY)] * 4,
            out_specs=(pl.BlockSpec(memory_space=vm),) * 2,
            scratch_shapes=scratch,
            compiler_params=pltpu.CompilerParams(
                collective_id=0, has_side_effects=True, vmem_limit_bytes=52 << 20),
            name="selected_inverse",
        )(inverse_diag, sub_diag, arrow_rows, arrow_inverse)

    placed = P("chain", "tile", None)
    return jax.shard_map(
        on_device, mesh=mesh, in_specs=(placed, placed, placed, P()), out_specs=(placed, placed), check_vma=False)
```

time: 163 us -> 146 us (0.90)
  Pallas kernels: 155 us -> 139 us
    pallas_call x1, Pallas kernels: 155 us -> 139 us  [on_device(): pl.pallas_call(functools.partial(kernel, planes, (row, node, panel, own_a...]
where the time goes in v2:
time: 146 us; the launch traced here: 144 us
  Pallas kernels  139 us (95%)
  local copies, waits for them, and re-layouts  4.64 us (3%)
    pallas_call x1, Pallas kernels, on_device(): pl.pallas_call(functools.partial(kernel, planes, (row, node, panel, own_a...  139 us
    unnamed x10, local copies, waits for them, and re-layouts  4.64 us

profile of v2, /device:TPU:32, one launch (start us, length us, event | category | flops | bytes accessed | tf_op | source)
XLA Modules:
  0.0 144.0 jit_solution(10196143920805571290)
XLA Ops:
  0.6 0.0 copy-start
  0.6 0.9 copy-done
  1.5 0.0 copy-start.1
  1.5 0.9 copy-done.1
  2.5 0.0 copy-start.2
  2.5 0.8 copy-done.2
  3.2 0.0 copy-start.3
  3.2 0.7 copy-done.3
  3.9 138.7 %selected_inverse.1 = (f32[2,48,768]{2,1,0:T(8,128)S(1)}, f32[2,8,768]{2,1,0:T(8,128)S(1)}) custom-call(bf16[2,48,768]{2,1,0:T(8,128)(2,1)S(1)} %copy-done, bf16[2,48,768]{2,1,0:T(8,128)(2,1)S(1)} %copy-done.1, bf16[2,8,768]{2,1,0:T(8,128)(2,1)S(1)} %copy-done.3, bf16[128,128]{1,0:T(8,128)(2,1)S(1)} %copy-done.2), custom_call_target="tpu_custom_call" | custom-call | tf_op jit(solution)/shard_map/selected_inverse/pallas_call | solution.py:664
  142.6 0.7 copy.8
  143.3 0.6 copy.9
Async XLA Ops:
  0.6 0.9 copy-start
  1.5 0.9 copy-start.1
  2.5 0.8 copy-start.2
  3.2 0.7 copy-start.3

commit v3 on v2

v3 whole, which is shorter than its diff:
```python
import functools
import jax
import jax.numpy as jnp
from jax import lax
from jax.experimental import pallas as pl
from jax.experimental.pallas import tpu as pltpu
from jax.sharding import PartitionSpec as P

MESH = pl.DeviceIdType.MESH
BF, F32 = jnp.bfloat16, jnp.float32
SIDE = 4
ODD, PAIR, PLANE, TRIPLE, EVEN, TWO, THREE, FOUR = range(8)
LONG = 7
OFFSETS = [(dy, dx) for dy in range(SIDE) for dx in range(SIDE) if dy or dx]
OFFSETS.sort(key=lambda o: min(o[0], 4 - o[0]) + min(o[1], 4 - o[1]))
RING = (1, 3, 2)
FAN = (2, 1, 3, 0)


def tdot(a, b):
    return lax.dot_general(a, b, (((0,), (0,)), ((), ())), preferred_element_type=F32)


def dot(a, b):
    return jnp.dot(a, b, preferred_element_type=F32)


def kernel(
    planes, sizes,
    l_in, b_in, a_in, z_in, diag_ref, arrow_ref,
    l_ref, b_ref, a_ref, z_ref, full_l, full_b, full_a, both_a, wide, wide_d, arrows_all, own_tiles, even, odd_far,
    cols, rows, tile, q_tile, m_tile, far_map, far_diag, part_out, part_in, part_own, part_sum, q_send,
    a_map, a_diag, b_arrow, b_diag, m_row, m_col, m_total, x_send, x_in, weight, out_send, out_in, sigma,
    send_sem, recv_sem, l_send, l_recv, load_sem,
):
    row, node, panel, own_arrow = sizes
    arrow = own_arrow * SIDE
    chain = lax.axis_index("chain")
    t = lax.axis_index("tile")
    z, core = chain // 2, chain % 2
    y, x = t // SIDE, t % SIDE
    r, c = jnp.where(core == 0, y, x), jnp.where(core == 0, x, y)
    widths = [min(node, -(-panel * (i + 1) // 128) * 128) for i in range(SIDE)]
    loads = [pltpu.make_async_copy(src, dst, load_sem.at[n]) for n, (src, dst) in enumerate(
        ((l_in, l_ref), (b_in, b_ref), (a_in, a_ref), (z_in, z_ref)))]
    for load in loads:
        load.start()

    def place(core, r, c):
        return jnp.where(core == 0, r * SIDE + c, c * SIDE + r)

    def dev(dz=0, dcore=0, dr=0, dc=0):
        zz = lax.rem(z + dz + planes, planes)
        cc = lax.rem(core + dcore, 2)
        return (zz * 2 + cc, place(cc, lax.rem(r + dr, SIDE), lax.rem(c + dc, SIDE)))

    def near_by(dy, dx):
        return (chain, lax.rem(y + dy, SIDE) * SIDE + lax.rem(x + dx, SIDE))

    r_at, c_at = [lax.rem(r + d, SIDE) for d in range(SIDE)], [lax.rem(c + d, SIDE) for d in range(SIDE)]
    r_dev, c_dev = [dev(dr=d) for d in range(SIDE)], [dev(dc=d) for d in range(SIDE)]
    is_first = core == 0
    has = [None] + [z + n < planes for n in (1, 2, 3)]
    has_a, has_b = has[1], z + 5 < planes
    late = []

    used = [0]

    def take(n):
        used[0] += n
        assert used[0] <= send_sem.shape[0]
        return used[0] - n

    def copy(src, dst, sem, where):
        return pltpu.make_async_remote_copy(
            src_ref=src, dst_ref=dst, send_sem=send_sem.at[sem], recv_sem=recv_sem.at[sem],
            device_id=where, device_id_type=MESH)

    class Gather:
        def __init__(self, buf, along_c, when=None):
            self.buf, self.along_c, self.base = buf, along_c, take(3)
            late.append((when, self))

        def each(self, arriving):
            at, where = (c_at, c_dev) if self.along_c else (r_at, r_dev)
            for n, d in enumerate(RING):
                to = at[SIDE - d] if arriving else at[0]
                yield copy(self.buf(at[0]), self.buf(to), self.base + n, where[d])

        def start(self):
            for move in self.each(False):
                move.start()

        def wait(self):
            for move in self.each(True):
                move.wait_recv()

    barrier = pltpu.get_barrier_semaphore()
    group = [near_by(dy, dx) for dy, dx in OFFSETS]
    first = [dev(dcore=1, dc=d) for d in range(SIDE)] + [dev(dz=d) for d in (1, 2, 3, -3)]
    second = [dev(dz=d, dcore=1) for d in (1, -3)]
    for peer in group:
        pl.semaphore_signal(barrier, inc=1, device_id=peer, device_id_type=MESH)
    for k, others in enumerate((first, second)):
        @pl.when(core == k)
        def _():
            for peer in others:
                pl.semaphore_signal(barrier, inc=1, device_id=peer, device_id_type=MESH)

    my_rows = pl.ds(pl.multiple_of(t * row, 16), row)
    panel_rows = pl.ds(pl.multiple_of(x * row, 16), row)
    mine = c // 2 == core
    block = lax.rem(c, 2)
    for i in range(SIDE - 1):
        if widths[i] < node:
            full_l[panel * i:panel * (i + 1), widths[i]:] = jnp.zeros((panel, node - widths[i]), BF)
    for load in loads:
        load.wait()
    both_a[...] = jnp.concatenate([a_ref[0].astype(F32), a_ref[1].astype(F32)], axis=0).astype(BF)
    for k, extra in enumerate((6, SIDE)):
        @pl.when(core == k)
        def _():
            pl.semaphore_wait(barrier, len(group) + extra)

    def to_column(b, row):
        return (chain, place(core, row, 2 * core + b))

    def l_copy(b, dr, w):
        return pltpu.make_async_remote_copy(
            src_ref=l_ref.at[b, :, :w], dst_ref=full_l.at[my_rows, :w], send_sem=l_send.at[b, dr],
            recv_sem=l_recv.at[t], device_id=to_column(b, lax.rem(r + dr, SIDE)), device_id_type=MESH)

    def b_copy(b):
        return pltpu.make_async_remote_copy(
            src_ref=b_ref.at[b], dst_ref=full_b.at[panel_rows], send_sem=l_send.at[b, 4],
            recv_sem=l_recv.at[16 + x], device_id=to_column(b, y), device_id_type=MESH)

    def a_copy(b):
        return pltpu.make_async_remote_copy(
            src_ref=both_a, dst_ref=full_a.at[x], send_sem=l_send.at[b, 5],
            recv_sem=l_recv.at[20 + x], device_id=to_column(b, y), device_id_type=MESH)

    def spread(do):
        for b in range(2):
            for i in range(SIDE):
                @pl.when(y == i)
                def _():
                    for dr in (1, 3, 2):
                        do(l_copy(b, dr, widths[i]))

            @pl.when(c != 2 * core + b)
            def _():
                for i in range(SIDE):
                    @pl.when(y == i)
                    def _():
                        do(l_copy(b, 0, widths[i]))

            @pl.when((c != 2 * core + b) | (r != y))
            def _():
                do(b_copy(b))
                do(a_copy(b))

    spread(lambda move: move.start())
    sigma[...] = tdot(z_ref[...], z_ref[...])
    tile_base = take(3)

    def tile_send(b, n):
        to = c_at[RING[n]]
        dst = odd_far.at[to] if b else even
        return pltpu.make_async_remote_copy(
            src_ref=own_tiles.at[to], dst_ref=dst, send_sem=send_sem.at[tile_base + n],
            recv_sem=l_recv.at[24 + b], device_id=c_dev[RING[n]], device_id_type=MESH)

    @pl.when(mine)
    def _():
        for b in range(2):
            @pl.when(block == b)
            def _():
                full_l[my_rows, :] = l_ref[b]

                @pl.when(r == y)
                def _():
                    full_b[panel_rows, :] = b_ref[b]
                    full_a[x] = both_a[...]
        for s in range(SIDE * SIDE):
            @pl.when(t != s)
            def _():
                w = widths[s // SIDE]
                pltpu.make_async_remote_copy(
                    src_ref=l_ref.at[0, :, :w], dst_ref=full_l.at[pl.ds(s * row, row), :w],
                    send_sem=l_send.at[0, 0], recv_sem=l_recv.at[s], device_id=c_dev[1], device_id_type=MESH,
                ).wait_recv()
        for s in range(SIDE):
            @pl.when((x != s) | (r != y))
            def _():
                pltpu.make_async_remote_copy(
                    src_ref=b_ref.at[0], dst_ref=full_b.at[pl.ds(s * row, row)], send_sem=l_send.at[0, 4],
                    recv_sem=l_recv.at[16 + s], device_id=c_dev[1], device_id_type=MESH).wait_recv()
                pltpu.make_async_remote_copy(
                    src_ref=both_a, dst_ref=full_a.at[s], send_sem=l_send.at[0, 5],
                    recv_sem=l_recv.at[20 + s], device_id=c_dev[1], device_id_type=MESH).wait_recv()
        for j in range(0, node, 256):
            wide[:panel, j:j + 256] = -dot(full_b[:, j:], full_l[j:, j:j + 256])
            arrows_all[:, j:j + 256] = -dot(full_a[...].reshape(SIDE * 2 * own_arrow, node)[:, j:], full_l[j:, j:j + 256])
        for i in range(SIDE):
            lo = pl.multiple_of(2 * own_arrow * i + own_arrow * block, 8)
            wide[panel + own_arrow * i:panel + own_arrow * (i + 1)] = arrows_all[pl.ds(lo, own_arrow)]
        for i in range(SIDE):
            @pl.when(r == i)
            def _():
                lo = panel * i
                wide_d[...] = tdot(full_l[lo:, lo:lo + panel], full_l[lo:, :])
        for i in range(SIDE):
            own_tiles[i, :panel + arrow] = wide[:, panel * i:panel * (i + 1)].astype(BF)
            own_tiles[i, panel + arrow:] = wide_d[:, panel * i:panel * (i + 1)].astype(BF)
        for b in range(2):
            @pl.when(block == b)
            def _():
                for n in range(3):
                    tile_send(b, n).start()
                if b:
                    odd_far[c] = own_tiles[c]
                else:
                    even[...] = own_tiles[c]

    def get_cols(slot, when=None):
        return Gather(lambda i: cols.at[slot, i], False, when)

    def get_rows(slot, when=None):
        return Gather(lambda i: rows.at[slot, i], True, when)

    def product(left, slot):
        total = dot(left(0), cols[slot, 0])
        for k in range(1, SIDE):
            total += dot(left(k), cols[slot, k])
        return total

    def new_map(left, near, to, spread=True):
        total = product(left, near)
        arrows = total[panel:] + m_tile[near]
        m_tile[to] = arrows
        tile[to, :panel] = total[:panel].astype(BF)
        tile[to, panel:] = arrows.astype(BF)
        if spread:
            cols[to, r] = total[:panel].astype(BF)
            rows[to, c] = total[:panel].astype(BF)

    class Congruence:
        def __init__(self, index, when=None):
            self.index, self.base = index, take(3)
            late.append((when, self))

        def each(self, arriving):
            for n, d in enumerate(RING):
                at = r_at[SIDE - d] if arriving else r
                yield copy(part_out.at[self.index, r_at[d]], part_in.at[self.index, at], self.base + n, r_dev[d])

        def add(self, left, near, first):
            right = product(left, near).astype(BF)
            for s in range(SIDE):
                piece = tdot(rows[near, s], right)
                part_sum[s] = piece if first else part_sum[s] + piece

        def send(self):
            for s in range(SIDE):
                part_out[self.index, s] = part_sum[s].astype(BF)
            for move in self.each(False):
                move.start()
            part_own[self.index] = part_sum[r]

        def start(self, left, near):
            self.add(left, near, True)
            self.send()

        def finish(self, near, to):
            total = part_own[self.index] + q_tile[near]
            for move in self.each(True):
                move.wait_recv()
            for d in RING:
                total += part_in[self.index, r_at[d]].astype(F32)
            q_tile[to] = total
            q_send[to] = total.astype(BF)

    for b in (1, 0):
        @pl.when(c != 2 * core + b)
        def _():
            pltpu.make_async_remote_copy(
                src_ref=own_tiles.at[0], dst_ref=odd_far.at[c] if b else even, send_sem=send_sem.at[tile_base],
                recv_sem=l_recv.at[24 + b], device_id=c_dev[1], device_id_type=MESH).wait_recv()
    cols[EVEN, r] = even[:panel]
    rows[EVEN, c] = even[:panel]
    even_cols, even_rows, odd_cols = get_cols(EVEN), get_rows(EVEN), get_cols(ODD)
    odd_panel = Gather(lambda i: odd_far.at[i, pl.ds(0, panel + arrow)], True)
    odd_diags = Gather(lambda i: odd_far.at[i, pl.ds(panel + arrow, panel)], True)
    even_cols.start()
    odd_panel.start()
    odd_diags.start()
    even_rows.start()
    cols[ODD, r] = odd_far[c, :panel]
    m_tile[EVEN] = even[panel:panel + arrow].astype(F32)
    q_tile[EVEN] = even[panel + arrow:].astype(F32)
    m_tile[ODD] = odd_far[c, panel:panel + arrow].astype(F32)
    q_tile[ODD] = odd_far[c, panel + arrow:].astype(F32)
    even_cols.wait()
    odd_panel.wait()
    new_map(lambda k: odd_far[k, :panel + arrow], EVEN, PAIR)
    fan = take(8)

    def fan_copy(d, diag):
        src = q_send.at[PAIR] if diag else tile.at[PAIR]
        dst = far_diag.at[0, c] if diag else far_map.at[0, c]
        return copy(src, dst, fan + 4 * diag + d, dev(dcore=1, dc=d))

    def fan_wait(diag):
        for d in range(SIDE):
            at = c_at[-d]
            src = q_send.at[PAIR] if diag else tile.at[PAIR]
            dst = far_diag.at[0, at] if diag else far_map.at[0, at]
            copy(src, dst, fan + 4 * diag + d, dev(dcore=1, dc=d)).wait_recv()

    @pl.when(core == 1)
    def _():
        for d in FAN:
            fan_copy(d, 0).start()

    pair_cols, pair_rows = get_cols(PAIR), get_rows(PAIR)
    pair = Congruence(0)

    @pl.when(is_first)
    def _():
        pair_cols.start()

    odd_diags.wait()
    even_rows.wait()
    pair.start(lambda k: odd_far[k, panel + arrow:], EVEN)

    @pl.when(is_first)
    def _():
        pair_rows.start()

    for k in range(SIDE):
        rows[ODD, k] = odd_far[k, :panel]

    z_base = take(6)

    def z_map(n):
        steps = (1, 1, 2)[n]
        src = tile.at[TWO if n else PLANE]
        return steps, copy(src, far_map.at[n + 1, c], z_base + n, dev(dz=-steps))

    def z_diag(n):
        return n, copy(q_send.at[PLANE], far_diag.at[n, c], z_base + 2 + n, dev(dz=-n))

    def z_each(copies, do):
        for steps, move in copies:
            @pl.when(z >= steps)
            def _():
                do(move)

    last_base = take(8)

    def last_copy(far, to_core, diag):
        if far:
            src = q_send.at[FOUR] if diag else tile.at[FOUR, pl.ds(panel, arrow)]
            dst = b_diag.at[c] if diag else b_arrow.at[c]
        else:
            src = q_send.at[FOUR] if diag else tile.at[FOUR]
            dst = a_diag.at[c] if diag else a_map.at[c]
        return copy(src, dst, last_base + 4 * far + 2 * to_core + diag, dev(dz=-5 if far else -1, dcore=to_core))

    def last_each(diag, do):
        for far, steps in ((0, 1), (1, 5)):
            @pl.when(z >= steps)
            def _():
                for k in range(2):
                    do(last_copy(far, k, diag))

    def last_wait(far, diag):
        for k in range(2):
            @pl.when(core == k)
            def _():
                last_copy(far, k, diag).wait_recv()

    far_maps = [None] + [Gather(lambda i, n=n: far_map.at[n, i], True, is_first & has[m]) for n, m in ((1, 1), (2, 3), (3, 2))]
    far_diags = [None] + [Gather(lambda i, n=n: far_diag.at[n, i], True, is_first & has[n]) for n in (1, 2, 3)]
    triple_cols, triple_rows = get_cols(TRIPLE, is_first), get_rows(TRIPLE, is_first)
    near = (None, PLANE, TWO, THREE)
    scan_when = (None, is_first, is_first & has[2], is_first & has[3])
    scan_cols = [None] + [get_cols(near[n], scan_when[n]) for n in (1, 2, 3)]
    scan_rows = [None] + [get_rows(near[n], scan_when[n]) for n in (1, 2, 3)]
    plane, triple, scan = Congruence(2, is_first), Congruence(1, is_first), Congruence(3, is_first & has_a)
    get_am = Gather(lambda i: a_map.at[i], True, has_a)
    get_bm = Gather(lambda i: b_arrow.at[i], True, has_b)
    get_aq = Gather(lambda i: a_diag.at[i], True, has_a)
    get_bq = Gather(lambda i: b_diag.at[i], True, has_b)
    long_cols, long_rows = [get_cols(LONG + j, has_b) for j in range(2)], [get_rows(LONG + j, has_b) for j in range(2)]
    finals = (jnp.where(core == 0, PLANE, PAIR), jnp.where(core == 0, TRIPLE, ODD))

    @pl.when(core == 1)
    def _():
        pair.finish(EVEN, PAIR)
        for d in FAN:
            fan_copy(d, 1).start()
        pair_cols.start()
        odd_cols.start()
        pair_rows.start()
        pair_cols.wait()
        pair_rows.wait()
        odd_cols.wait()

    @pl.when(core == 0)
    def _():
        fan_wait(0)
        pair_cols.wait()
        new_map(lambda k: far_map[0, k], PAIR, PLANE)
        z_each([z_map(0)], lambda move: move.start())
        scan_cols[1].start()
        pair.finish(EVEN, PAIR)

        @pl.when(has[1])
        def _():
            z_map(0)[1].wait_recv()
            far_maps[1].start()

        scan_rows[1].start()
        pair_rows.wait()
        fan_wait(1)
        plane.start(lambda k: far_diag[0, k], PAIR)
        scan_cols[1].wait()

        @pl.when(has[1])
        def _():
            far_maps[1].wait()
            new_map(lambda k: far_map[1, k], PLANE, TWO)

        @pl.when(z + 1 == planes)
        def _():
            tile[TWO] = tile[PLANE]

        z_each([z_map(1), z_map(2)], lambda move: move.start())

        @pl.when(has[2])
        def _():
            scan_cols[2].start()

        odd_cols.start()
        plane.finish(PAIR, PLANE)
        z_each([z_diag(n) for n in (1, 2, 3)], lambda move: move.start())

        @pl.when(has[2])
        def _():
            scan_rows[2].start()

        odd_cols.wait()
        new_map(lambda k: far_map[0, k], ODD, TRIPLE)
        triple_cols.start()

        @pl.when(has[1])
        def _():
            z_map(1)[1].wait_recv()

        @pl.when(has[3])
        def _():
            far_maps[2].start()

        @pl.when(has[2])
        def _():
            z_map(2)[1].wait_recv()
            far_maps[3].start()

        triple.start(lambda k: far_diag[0, k], ODD)

        for n in (1, 2, 3):
            @pl.when(has[n])
            def _():
                z_diag(n)[1].wait_recv()
                far_diags[n].start()

        @pl.when(has[2])
        def _():
            scan_cols[2].wait()
            far_maps[3].wait()
            new_map(lambda k: far_map[3, k], TWO, FOUR, False)

        @pl.when(z + 2 >= planes)
        def _():
            tile[FOUR] = tile[TWO]

        last_each(0, lambda move: move.start())

        @pl.when(has[3])
        def _():
            far_maps[2].wait()
            new_map(lambda k: far_map[2, k], PLANE, THREE)
            scan_cols[3].start()
            scan_rows[3].start()

        triple_rows.start()
        scan_rows[1].wait()

        @pl.when(has[1])
        def _():
            far_diags[1].wait()
            scan.add(lambda k: far_diag[1, k], PLANE, True)

        @pl.when(has[2])
        def _():
            scan_rows[2].wait()
            far_diags[2].wait()
            scan.add(lambda k: far_diag[2, k], TWO, False)

        triple_cols.wait()

    @pl.when(has_a)
    def _():
        last_wait(0, 0)
        get_am.start()

    @pl.when(has_b)
    def _():
        last_wait(1, 0)
        get_bm.start()

    @pl.when((core == 0) & has_a)
    def _():
        @pl.when(has[3])
        def _():
            far_diags[3].wait()
            scan_cols[3].wait()
            scan_rows[3].wait()
            scan.add(lambda k: far_diag[3, k], THREE, False)
        scan.send()

    @pl.when((core == 0) & (z + 1 == planes))
    def _():
        q_send[FOUR] = q_send[PLANE]
        last_each(1, lambda move: move.start())

    @pl.when(has_a)
    def _():
        get_am.wait()
        for j in range(2):
            total = product(lambda k: a_map[k], finals[j])
            m_total[j] = total[panel:] + m_tile[finals[j]]

            @pl.when(has_b)
            def _():
                cols[LONG + j, r] = total[:panel].astype(BF)
                rows[LONG + j, c] = total[:panel].astype(BF)
                long_cols[j].start()

        @pl.when(has_b)
        def _():
            for j in range(2):
                long_rows[j].start()

    @pl.when(z + 1 == planes)
    def _():
        for j in range(2):
            m_total[j] = m_tile[finals[j]]

    @pl.when(core == 0)
    def _():
        @pl.when(has_a)
        def _():
            scan.finish(PLANE, FOUR)
            last_each(1, lambda move: move.start())
        triple.finish(ODD, TRIPLE)
        triple_rows.wait()

    @pl.when(has_a)
    def _():
        last_wait(0, 1)
        get_aq.start()

    @pl.when(has_b)
    def _():
        last_wait(1, 1)
        get_bq.start()

    @pl.when(has_b)
    def _():
        get_bm.wait()
        for j in range(2):
            long_cols[j].wait()
            m_total[j] += product(lambda k: b_arrow[k], LONG + j)

    get_mr, get_mc = [], []
    for j in range(2):
        m_row[j, c] = m_total[j].astype(BF)
        m_col[j, r] = m_total[j].astype(BF)
        get_mr.append(Gather(lambda i, j=j: m_row.at[j, i], True))
        get_mc.append(Gather(lambda i, j=j: m_col.at[j, i], False))
        get_mr[j].start()
        get_mc[j].start()

    @pl.when(has_a)
    def _():
        get_aq.wait()
        for j in range(2):
            weight[j] = product(lambda k: a_diag[k], finals[j]).astype(BF)

    x_base = take(2 * SIDE)

    def x_out(j, do):
        for sub in range(SIDE):
            @pl.when((r != y) | (x != sub))
            def _():
                do(pltpu.make_async_remote_copy(
                    src_ref=x_send.at[j, own_arrow * sub:own_arrow * (sub + 1)], dst_ref=x_in.at[j, c],
                    send_sem=send_sem.at[x_base + SIDE * j + sub], recv_sem=recv_sem.at[x_base + SIDE * j + c],
                    device_id=(chain, r * SIDE + sub), device_id_type=MESH))

    def x_wait(j):
        for i in range(SIDE):
            @pl.when((r != y) | (c != i))
            def _():
                copy(x_send.at[j, :own_arrow], x_in.at[j, i], x_base + SIDE * j + i, c_dev[1]).wait_recv()

    sigma_rows = sigma[pl.ds(pl.multiple_of(r * arrow, 8), arrow)]
    for j in range(2):
        get_mr[j].wait()
        get_mc[j].wait()
        x_send[j] = lax.dot_general(
            sigma_rows, m_col[j].reshape(SIDE * arrow, panel).astype(F32), (((1,), (0,)), ((), ())),
            precision=lax.Precision.HIGHEST, preferred_element_type=F32)

        @pl.when(r == y)
        def _():
            x_in[j, c] = x_send[j, pl.ds(pl.multiple_of(x * own_arrow, 8), own_arrow)]
        x_out(j, lambda move: move.start())

    @pl.when(has_b)
    def _():
        get_bq.wait()
        for j in range(2):
            long_rows[j].wait()
            weight[2 + j] = product(lambda k: b_diag[k], LONG + j).astype(BF)

    out_base = take(2 * len(OFFSETS))

    def out_each(j, arriving):
        for n, (dy, dx) in enumerate(OFFSETS):
            ty, tx = lax.rem(y + dy, SIDE), lax.rem(x + dx, SIDE)
            sy, sx = lax.rem(y + SIDE - dy, SIDE), lax.rem(x + SIDE - dx, SIDE)
            at = (jnp.where(core == 0, sy, sx), jnp.where(core == 0, sx, sy)) if arriving else (r, c)
            src = out_send.at[j, ty, pl.ds(pl.multiple_of(tx * row, 16), row)]
            yield copy(src, out_in.at[j, at[0], at[1]], out_base + len(OFFSETS) * j + n, near_by(dy, dx))

    for j in range(2):
        arrows = x_send[j].astype(BF)
        for s in range(SIDE):
            part_own[5] = tdot(m_row[j, s], arrows)

            @pl.when(has_a)
            def _():
                part_own[5] += tdot(rows[finals[j], s], weight[j])

            @pl.when(has_b)
            def _():
                part_own[5] += tdot(rows[LONG + j, s], weight[2 + j])

            @pl.when(r == s)
            def _():
                part_own[5] += q_tile[finals[j]]
            out_send[j, s] = part_own[5].astype(BF)
        out_in[j, r, c] = out_send[j, y, pl.ds(pl.multiple_of(x * row, 16), row)]
        for move in out_each(j, False):
            move.start()
    groups = {}
    for when, sender in late:
        groups.setdefault(id(when), (when, []))[1].append(sender)

    def all_sent(senders):
        for sender in senders:
            for move in sender.each(False):
                move.wait_send()

    for when, senders in groups.values():
        if when is None:
            all_sent(senders)
        else:
            pl.when(when)(lambda senders=senders: all_sent(senders))
    spread(lambda move: move.wait_send())

    @pl.when(mine)
    def _():
        for n in range(3):
            tile_send(0, n).wait_send()

    @pl.when(core == 1)
    def _():
        for d in FAN:
            fan_copy(d, 0).wait_send()
            fan_copy(d, 1).wait_send()

    @pl.when(core == 0)
    def _():
        z_each([z_map(n) for n in range(3)] + [z_diag(n) for n in (1, 2, 3)], lambda move: move.wait_send())
        last_each(0, lambda move: move.wait_send())
        last_each(1, lambda move: move.wait_send())

    for j in range(2):
        x_wait(j)
        for i in range(SIDE):
            arrow_ref[j, :, panel * i:panel * (i + 1)] = x_in[j, i]
        x_out(j, lambda move: move.wait_send())
    for j in range(2):
        for move in out_each(j, True):
            move.wait_recv()
        for i in range(SIDE):
            total = out_in[j, 0, i].astype(F32)
            for k in range(1, SIDE):
                total += out_in[j, k, i].astype(F32)
            diag_ref[j, :, panel * i:panel * (i + 1)] = total
    for j in range(2):
        for move in out_each(j, False):
            move.wait_send()


def solution(mesh):
    planes = mesh.shape["chain"] // 2

    def on_device(inverse_diag, sub_diag, arrow_rows, arrow_inverse):
        count, row, node = inverse_diag.shape
        own_arrow = arrow_rows.shape[1]
        panel, arrow = row * SIDE, own_arrow * SIDE
        vm = pltpu.VMEM
        scratch = [
            vm(inverse_diag.shape, BF), vm(sub_diag.shape, BF), vm(arrow_rows.shape, BF), vm(arrow_inverse.shape, BF),
            vm((node, node), BF), vm((panel, node), BF), vm((SIDE, 2 * own_arrow, node), BF), vm((2 * own_arrow, node), BF),
            vm((panel + arrow, node), F32), vm((panel, node), F32), vm((2 * arrow, node), F32),
            vm((SIDE, 2 * panel + arrow, panel), BF), vm((2 * panel + arrow, panel), BF),
            vm((SIDE, 2 * panel + arrow, panel), BF),
            vm((9, SIDE, panel, panel), BF), vm((9, SIDE, panel, panel), BF),
            vm((8, panel + arrow, panel), BF), vm((8, panel, panel), F32), vm((8, arrow, panel), F32),
            vm((4, SIDE, panel + arrow, panel), BF), vm((4, SIDE, panel, panel), BF),
            vm((5, SIDE, panel, panel), BF), vm((5, SIDE, panel, panel), BF), vm((6, panel, panel), F32),
            vm((SIDE, panel, panel), F32),
            vm((8, panel, panel), BF),
            vm((SIDE, panel + arrow, panel), BF), vm((SIDE, panel, panel), BF),
            vm((SIDE, arrow, panel), BF), vm((SIDE, panel, panel), BF),
            vm((2, SIDE, arrow, panel), BF), vm((2, SIDE, arrow, panel), BF), vm((2, arrow, panel), F32),
            vm((2, arrow, panel), F32), vm((2, SIDE, own_arrow, panel), F32),
            vm((4, panel, panel), BF), vm((2, SIDE, panel, panel), BF), vm((2, SIDE, SIDE, row, panel), BF),
            vm(arrow_inverse.shape, F32),
            pltpu.SemaphoreType.DMA((200,)), pltpu.SemaphoreType.DMA((200,)),
            pltpu.SemaphoreType.DMA((2, 6)), pltpu.SemaphoreType.DMA((26,)), pltpu.SemaphoreType.DMA((4,)),
        ]
        return pl.pallas_call(
            functools.partial(kernel, planes, (row, node, panel, own_arrow)),
            out_shape=(
                jax.ShapeDtypeStruct(inverse_diag.shape, F32),
                jax.ShapeDtypeStruct(arrow_rows.shape, F32),
            ),
            in_specs=[pl.BlockSpec(memory_space=pl.ANY)] * 4,
            out_specs=(pl.BlockSpec(memory_space=vm),) * 2,
            scratch_shapes=scratch,
            compiler_params=pltpu.CompilerParams(
                collective_id=0, has_side_effects=True, vmem_limit_bytes=62 << 20),
            name="selected_inverse",
        )(inverse_diag, sub_diag, arrow_rows, arrow_inverse)

    placed = P("chain", "tile", None)
    return jax.shard_map(
        on_device, mesh=mesh, in_specs=(placed, placed, placed, P()), out_specs=(placed, placed), check_vma=False)
```

time: 146 us -> 138 us (0.945)
  Pallas kernels: 139 us -> 134 us
  local copies, waits for them, and re-layouts: 4.64 us -> 2.33 us
    pallas_call x1, Pallas kernels: 139 us -> 134 us  [on_device(): pl.pallas_call(functools.partial(kernel, planes, (row, node, panel, own_a...]
    unnamed x10 -> x4, local copies, waits for them, and re-layouts: 4.64 us -> 2.33 us
where the time goes in v3:
time: 138 us; the launch traced here: 137 us
  Pallas kernels  134 us (97%)
  local copies, waits for them, and re-layouts  2.33 us (2%)
    pallas_call x1, Pallas kernels, on_device(): pl.pallas_call(functools.partial(kernel, planes, (row, node, panel, own_a...  134 us

profile of v3, /device:TPU:32, one launch (start us, length us, event | category | flops | bytes accessed | tf_op | source)
XLA Modules:
  0.0 137.0 jit_solution(3085517638550647136)
XLA Ops:
  0.6 134.0 %selected_inverse.1 = (f32[2,48,768]{2,1,0:T(8,128)}, f32[2,8,768]{2,1,0:T(8,128)}) custom-call(bf16[2,48,768]{2,1,0:T(8,128)(2,1)} %l_in.1, bf16[2,48,768]{2,1,0:T(8,128)(2,1)} %b_in.1, bf16[2,8,768]{2,1,0:T(8,128)(2,1)} %a_in.1, bf16[128,128]{1,0:T(8,128)(2,1)} %z_in.1), custom_call_target="tpu_custom_call" | custom-call | tf_op jit(solution)/shard_map/selected_inverse/pallas_call | solution.py:750
  134.6 0.0 copy-start
  134.6 1.7 %copy.8 = f32[2,48,768]{2,1,0:T(8,128)} copy(f32[2,48,768]{2,1,0:T(8,128)} %get-tuple-element.4) | data formatting | bytes 589824
  136.4 0.0 copy-done
  136.4 0.6 copy.9
Async XLA Ops:
  134.6 1.7 %copy-start = (f32[2,8,768]{2,1,0:T(8,128)S(1)}, f32[2,8,768]{2,1,0:T(8,128)}, u32[]{:S(2)}) copy-start(f32[2,8,768]{2,1,0:T(8,128)} %get-tuple-element.5) | copy-start | bytes 147460

commit v4 on v3

--- a/solution.py
+++ b/solution.py
@@ -30,7 +30,7 @@
     l_in, b_in, a_in, z_in, diag_ref, arrow_ref,
     l_ref, b_ref, a_ref, z_ref, full_l, full_b, full_a, both_a, wide, wide_d, arrows_all, own_tiles, even, odd_far,
     cols, rows, tile, q_tile, m_tile, far_map, far_diag, part_out, part_in, part_own, part_sum, q_send,
-    a_map, a_diag, b_arrow, b_diag, m_row, m_col, m_total, x_send, x_in, weight, out_send, out_in, sigma,
+    a_map, a_diag, b_arrow, b_diag, m_row, m_col, m_total, x_send, x_in, weight, last_sum, out_send, out_in, sigma,
     send_sem, recv_sem, l_send, l_recv, load_sem,
 ):
     row, node, panel, own_arrow = sizes
@@ -594,12 +594,6 @@
         get_mr[j].start()
         get_mc[j].start()
 
-    @pl.when(has_a)
-    def _():
-        get_aq.wait()
-        for j in range(2):
-            weight[j] = product(lambda k: a_diag[k], finals[j]).astype(BF)
-
     x_base = take(2 * SIDE)
 
     def x_out(j, do):
@@ -616,6 +610,20 @@
             @pl.when((r != y) | (c != i))
             def _():
                 copy(x_send.at[j, :own_arrow], x_in.at[j, i], x_base + SIDE * j + i, c_dev[1]).wait_recv()
+
+    for j in range(2):
+        @pl.when(has_a)
+        def _():
+            if j == 0:
+                get_aq.wait()
+            right = product(lambda k: a_diag[k], finals[j]).astype(BF)
+            for s in range(SIDE):
+                last_sum[j, s] = tdot(rows[finals[j], s], right)
+
+        @pl.when(z + 1 == planes)
+        def _():
+            last_sum[j] = jnp.zeros((SIDE, panel, panel), F32)
+        last_sum[j, r] += q_tile[finals[j]]
 
     sigma_rows = sigma[pl.ds(pl.multiple_of(r * arrow, 8), arrow)]
     for j in range(2):
@@ -629,44 +637,51 @@
         def _():
             x_in[j, c] = x_send[j, pl.ds(pl.multiple_of(x * own_arrow, 8), own_arrow)]
         x_out(j, lambda move: move.start())
-
-    @pl.when(has_b)
-    def _():
-        get_bq.wait()
-        for j in range(2):
-            long_rows[j].wait()
-            weight[2 + j] = product(lambda k: b_diag[k], LONG + j).astype(BF)
-
-    out_base = take(2 * len(OFFSETS))
-
-    def out_each(j, arriving):
-        for n, (dy, dx) in enumerate(OFFSETS):
-            ty, tx = lax.rem(y + dy, SIDE), lax.rem(x + dx, SIDE)
-            sy, sx = lax.rem(y + SIDE - dy, SIDE), lax.rem(x + SIDE - dx, SIDE)
-            at = (jnp.where(core == 0, sy, sx), jnp.where(core == 0, sx, sy)) if arriving else (r, c)
-            src = out_send.at[j, ty, pl.ds(pl.multiple_of(tx * row, 16), row)]
-            yield copy(src, out_in.at[j, at[0], at[1]], out_base + len(OFFSETS) * j + n, near_by(dy, dx))
-
-    for j in range(2):
         arrows = x_send[j].astype(BF)
         for s in range(SIDE):
-            part_own[5] = tdot(m_row[j, s], arrows)
-
-            @pl.when(has_a)
-            def _():
-                part_own[5] += tdot(rows[finals[j], s], weight[j])
+            last_sum[j, s] += tdot(m_row[j, s], arrows)
+
+    out_base = take(2 * SIDE * SIDE)
+
+    def out_copy(j, i, dx):
+        tx = lax.rem(x + dx, SIDE)
+        src = out_send.at[j, r_at[i], pl.ds(pl.multiple_of(tx * row, 16), row)]
+        sem = out_base + SIDE * SIDE * j
+        return pltpu.make_async_remote_copy(
+            src_ref=src, dst_ref=out_in.at[j, r, c], send_sem=send_sem.at[sem + SIDE * i + dx],
+            recv_sem=recv_sem.at[sem + t], device_id=(chain, r_at[i] * SIDE + tx), device_id_type=MESH)
+
+    def out_each(j, i, do):
+        for dx in (1, 3, 2):
+            do(out_copy(j, i, dx))
+
+        @pl.when(r_at[i] != y)
+        def _():
+            do(out_copy(j, i, 0))
+
+    @pl.when(has_b)
+    def _():
+        get_bq.wait()
+
+    for j in range(2):
+        @pl.when(has_b)
+        def _():
+            long_rows[j].wait()
+            weight[...] = product(lambda k: b_diag[k], LONG + j).astype(BF)
+
+        for i in (1, 2, 3, 0):
+            s = r_at[i]
 
             @pl.when(has_b)
             def _():
-                part_own[5] += tdot(rows[LONG + j, s], weight[2 + j])
-
-            @pl.when(r == s)
-            def _():
-                part_own[5] += q_tile[finals[j]]
-            out_send[j, s] = part_own[5].astype(BF)
+                out_send[j, s] = (last_sum[j, s] + tdot(rows[LONG + j, s], weight[...])).astype(BF)
+
+            @pl.when(z + 5 >= planes)
+            def _():
+                out_send[j, s] = last_sum[j, s].astype(BF)
+            out_each(j, i, lambda move: move.start())
         out_in[j, r, c] = out_send[j, y, pl.ds(pl.multiple_of(x * row, 16), row)]
-        for move in out_each(j, False):
-            move.start()
+
     groups = {}
     for when, sender in late:
         groups.setdefault(id(when), (when, []))[1].append(sender)
@@ -706,16 +721,21 @@
             arrow_ref[j, :, panel * i:panel * (i + 1)] = x_in[j, i]
         x_out(j, lambda move: move.wait_send())
     for j in range(2):
-        for move in out_each(j, True):
-            move.wait_recv()
+        for sy in range(SIDE):
+            for sx in range(SIDE):
+                @pl.when(t != SIDE * sy + sx)
+                def _():
+                    at = (jnp.where(is_first, sy, sx), jnp.where(is_first, sx, sy))
+                    copy(out_send.at[j, 0, :row], out_in.at[j, at[0], at[1]],
+                         out_base + SIDE * SIDE * j + SIDE * sy + sx, c_dev[1]).wait_recv()
         for i in range(SIDE):
             total = out_in[j, 0, i].astype(F32)
             for k in range(1, SIDE):
                 total += out_in[j, k, i].astype(F32)
             diag_ref[j, :, panel * i:panel * (i + 1)] = total
     for j in range(2):
-        for move in out_each(j, False):
-            move.wait_send()
+        for i in range(SIDE):
+            out_each(j, i, lambda move: move.wait_send())
 
 
 def solution(mesh):
@@ -742,9 +762,9 @@
             vm((SIDE, arrow, panel), BF), vm((SIDE, panel, panel), BF),
             vm((2, SIDE, arrow, panel), BF), vm((2, SIDE, arrow, panel), BF), vm((2, arrow, panel), F32),
             vm((2, arrow, panel), F32), vm((2, SIDE, own_arrow, panel), F32),
-            vm((4, panel, panel), BF), vm((2, SIDE, panel, panel), BF), vm((2, SIDE, SIDE, row, panel), BF),
+            vm((panel, panel), BF), vm((2, SIDE, panel, panel), F32), vm((2, SIDE, panel, panel), BF), vm((2, SIDE, SIDE, row, panel), BF),
             vm(arrow_inverse.shape, F32),
-            pltpu.SemaphoreType.DMA((200,)), pltpu.SemaphoreType.DMA((200,)),
+            pltpu.SemaphoreType.DMA((210,)), pltpu.SemaphoreType.DMA((210,)),
             pltpu.SemaphoreType.DMA((2, 6)), pltpu.SemaphoreType.DMA((26,)), pltpu.SemaphoreType.DMA((4,)),
         ]
         return pl.pallas_call(

time: 138 us -> 137 us (level)
  no operation moved by 1% of the time
where the time goes in v4:
time: 137 us
  Pallas kernels  134 us (98%)
  local copies, waits for them, and re-layouts  2.33 us (2%)
    pallas_call x1, Pallas kernels, on_device(): pl.pallas_call(functools.partial(kernel, planes, (row, node, panel, own_a...  134 us

profile of v4, /device:TPU:32, one launch (start us, length us, event | category | flops | bytes accessed | tf_op | source)
XLA Modules:
  0.0 136.5 jit_solution(18071767174251311961)
XLA Ops:
  0.6 133.5 %selected_inverse.1 = (f32[2,48,768]{2,1,0:T(8,128)}, f32[2,8,768]{2,1,0:T(8,128)}) custom-call(bf16[2,48,768]{2,1,0:T(8,128)(2,1)} %l_in.1, bf16[2,48,768]{2,1,0:T(8,128)(2,1)} %b_in.1, bf16[2,8,768]{2,1,0:T(8,128)(2,1)} %a_in.1, bf16[128,128]{1,0:T(8,128)(2,1)} %z_in.1), custom_call_target="tpu_custom_call" | custom-call | tf_op jit(solution)/shard_map/selected_inverse/pallas_call | solution.py:770
  134.2 0.0 copy-start
  134.2 1.7 %copy.8 = f32[2,48,768]{2,1,0:T(8,128)} copy(f32[2,48,768]{2,1,0:T(8,128)} %get-tuple-element.4) | data formatting | bytes 589824
  135.9 0.0 copy-done
  135.9 0.6 copy.9
Async XLA Ops:
  134.2 1.7 %copy-start = (f32[2,8,768]{2,1,0:T(8,128)S(1)}, f32[2,8,768]{2,1,0:T(8,128)}, u32[]{:S(2)}) copy-start(f32[2,8,768]{2,1,0:T(8,128)} %get-tuple-element.5) | copy-start | bytes 147460

commit v5 on v4

--- a/solution.py
+++ b/solution.py
@@ -13,7 +13,7 @@
 LONG = 7
 OFFSETS = [(dy, dx) for dy in range(SIDE) for dx in range(SIDE) if dy or dx]
 OFFSETS.sort(key=lambda o: min(o[0], 4 - o[0]) + min(o[1], 4 - o[1]))
-RING = (1, 3, 2)
+RING = (2, 1, 3)
 FAN = (2, 1, 3, 0)
 
 
@@ -145,7 +145,7 @@
             for i in range(SIDE):
                 @pl.when(y == i)
                 def _():
-                    for dr in (1, 3, 2):
+                    for dr in (2, 1, 3):
                         do(l_copy(b, dr, widths[i]))
 
             @pl.when(c != 2 * core + b)
@@ -162,14 +162,37 @@
 
     spread(lambda move: move.start())
     sigma[...] = tdot(z_ref[...], z_ref[...])
-    tile_base = take(3)
-
-    def tile_send(b, n):
-        to = c_at[RING[n]]
-        dst = odd_far.at[to] if b else even
+    tile_base = take(6)
+    tile_parts = (pl.ds(0, panel + arrow), pl.ds(panel + arrow, panel))
+
+    def tile_send(b, n, part):
+        to, at = c_at[RING[n]], tile_parts[part]
+        dst = odd_far.at[to, at] if b else even.at[at]
         return pltpu.make_async_remote_copy(
-            src_ref=own_tiles.at[to], dst_ref=dst, send_sem=send_sem.at[tile_base + n],
-            recv_sem=l_recv.at[24 + b], device_id=c_dev[RING[n]], device_id_type=MESH)
+            src_ref=own_tiles.at[to, at], dst_ref=dst, send_sem=send_sem.at[tile_base + 3 * part + n],
+            recv_sem=l_recv.at[24 + 2 * part + b], device_id=c_dev[RING[n]], device_id_type=MESH)
+
+    def tile_start(part):
+        at = tile_parts[part]
+        for b in range(2):
+            @pl.when(block == b)
+            def _():
+                for n in range(3):
+                    tile_send(b, n, part).start()
+                if b:
+                    odd_far[c, at] = own_tiles[c, at]
+                else:
+                    even[at] = own_tiles[c, at]
+
+    def tile_wait(part):
+        at = tile_parts[part]
+        for b in (1, 0):
+            @pl.when(c != 2 * core + b)
+            def _():
+                pltpu.make_async_remote_copy(
+                    src_ref=own_tiles.at[0, at], dst_ref=odd_far.at[c, at] if b else even.at[at],
+                    send_sem=send_sem.at[tile_base], recv_sem=l_recv.at[24 + 2 * part + b],
+                    device_id=c_dev[1], device_id_type=MESH).wait_recv()
 
     @pl.when(mine)
     def _():
@@ -206,22 +229,16 @@
             lo = pl.multiple_of(2 * own_arrow * i + own_arrow * block, 8)
             wide[panel + own_arrow * i:panel + own_arrow * (i + 1)] = arrows_all[pl.ds(lo, own_arrow)]
         for i in range(SIDE):
+            own_tiles[i, :panel + arrow] = wide[:, panel * i:panel * (i + 1)].astype(BF)
+        tile_start(0)
+        for i in range(SIDE):
             @pl.when(r == i)
             def _():
                 lo = panel * i
                 wide_d[...] = tdot(full_l[lo:, lo:lo + panel], full_l[lo:, :])
         for i in range(SIDE):
-            own_tiles[i, :panel + arrow] = wide[:, panel * i:panel * (i + 1)].astype(BF)
             own_tiles[i, panel + arrow:] = wide_d[:, panel * i:panel * (i + 1)].astype(BF)
-        for b in range(2):
-            @pl.when(block == b)
-            def _():
-                for n in range(3):
-                    tile_send(b, n).start()
-                if b:
-                    odd_far[c] = own_tiles[c]
-                else:
-                    even[...] = own_tiles[c]
+        tile_start(1)
 
     def get_cols(slot, when=None):
         return Gather(lambda i: cols.at[slot, i], False, when)
@@ -281,19 +298,15 @@
             q_tile[to] = total
             q_send[to] = total.astype(BF)
 
-    for b in (1, 0):
-        @pl.when(c != 2 * core + b)
-        def _():
-            pltpu.make_async_remote_copy(
-                src_ref=own_tiles.at[0], dst_ref=odd_far.at[c] if b else even, send_sem=send_sem.at[tile_base],
-                recv_sem=l_recv.at[24 + b], device_id=c_dev[1], device_id_type=MESH).wait_recv()
+    tile_wait(0)
     cols[EVEN, r] = even[:panel]
-    rows[EVEN, c] = even[:panel]
     even_cols, even_rows, odd_cols = get_cols(EVEN), get_rows(EVEN), get_cols(ODD)
     odd_panel = Gather(lambda i: odd_far.at[i, pl.ds(0, panel + arrow)], True)
     odd_diags = Gather(lambda i: odd_far.at[i, pl.ds(panel + arrow, panel)], True)
     even_cols.start()
     odd_panel.start()
+    rows[EVEN, c] = even[:panel]
+    tile_wait(1)
     odd_diags.start()
     even_rows.start()
     cols[ODD, r] = odd_far[c, :panel]
@@ -301,6 +314,7 @@
     q_tile[EVEN] = even[panel + arrow:].astype(F32)
     m_tile[ODD] = odd_far[c, panel:panel + arrow].astype(F32)
     q_tile[ODD] = odd_far[c, panel + arrow:].astype(F32)
+    odd_cols.start()
     even_cols.wait()
     odd_panel.wait()
     new_map(lambda k: odd_far[k, :panel + arrow], EVEN, PAIR)
@@ -369,7 +383,7 @@
         return copy(src, dst, last_base + 4 * far + 2 * to_core + diag, dev(dz=-5 if far else -1, dcore=to_core))
 
     def last_each(diag, do):
-        for far, steps in ((0, 1), (1, 5)):
+        for far, steps in ((1, 5), (0, 1)):
             @pl.when(z >= steps)
             def _():
                 for k in range(2):
@@ -402,7 +416,6 @@
         for d in FAN:
             fan_copy(d, 1).start()
         pair_cols.start()
-        odd_cols.start()
         pair_rows.start()
         pair_cols.wait()
         pair_rows.wait()
@@ -437,15 +450,14 @@
         def _():
             tile[TWO] = tile[PLANE]
 
-        z_each([z_map(1), z_map(2)], lambda move: move.start())
+        z_each([z_map(2), z_map(1)], lambda move: move.start())
 
         @pl.when(has[2])
         def _():
             scan_cols[2].start()
 
-        odd_cols.start()
         plane.finish(PAIR, PLANE)
-        z_each([z_diag(n) for n in (1, 2, 3)], lambda move: move.start())
+        z_each([z_diag(n) for n in (3, 2, 1)], lambda move: move.start())
 
         @pl.when(has[2])
         def _():
@@ -652,7 +664,7 @@
             recv_sem=recv_sem.at[sem + t], device_id=(chain, r_at[i] * SIDE + tx), device_id_type=MESH)
 
     def out_each(j, i, do):
-        for dx in (1, 3, 2):
+        for dx in (2, 1, 3):
             do(out_copy(j, i, dx))
 
         @pl.when(r_at[i] != y)
@@ -669,7 +681,7 @@
             long_rows[j].wait()
             weight[...] = product(lambda k: b_diag[k], LONG + j).astype(BF)
 
-        for i in (1, 2, 3, 0):
+        for i in (2, 1, 3, 0):
             s = r_at[i]
 
             @pl.when(has_b)
@@ -701,7 +713,8 @@
     @pl.when(mine)
     def _():
         for n in range(3):
-            tile_send(0, n).wait_send()
+            tile_send(0, n, 0).wait_send()
+            tile_send(0, n, 1).wait_send()
 
     @pl.when(core == 1)
     def _():
@@ -765,7 +778,7 @@
             vm((panel, panel), BF), vm((2, SIDE, panel, panel), F32), vm((2, SIDE, panel, panel), BF), vm((2, SIDE, SIDE, row, panel), BF),
             vm(arrow_inverse.shape, F32),
             pltpu.SemaphoreType.DMA((210,)), pltpu.SemaphoreType.DMA((210,)),
-            pltpu.SemaphoreType.DMA((2, 6)), pltpu.SemaphoreType.DMA((26,)), pltpu.SemaphoreType.DMA((4,)),
+            pltpu.SemaphoreType.DMA((2, 6)), pltpu.SemaphoreType.DMA((28,)), pltpu.SemaphoreType.DMA((4,)),
         ]
         return pl.pallas_call(
             functools.partial(kernel, planes, (row, node, panel, own_arrow)),

time: 137 us -> 130 us (0.949)
  Pallas kernels: 134 us -> 127 us
    pallas_call x1, Pallas kernels: 134 us -> 127 us  [on_device(): pl.pallas_call(functools.partial(kernel, planes, (row, node, panel, own_a...]
where the time goes in v5:
time: 130 us
  Pallas kernels  127 us (98%)
  local copies, waits for them, and re-layouts  2.33 us (2%)
    pallas_call x1, Pallas kernels, on_device(): pl.pallas_call(functools.partial(kernel, planes, (row, node, panel, own_a...  127 us

profile of v5, /device:TPU:32, one launch (start us, length us, event | category | flops | bytes accessed | tf_op | source)
XLA Modules:
  0.0 129.6 jit_solution(11257960590357460546)
XLA Ops:
  0.6 126.7 %selected_inverse.1 = (f32[2,48,768]{2,1,0:T(8,128)}, f32[2,8,768]{2,1,0:T(8,128)}) custom-call(bf16[2,48,768]{2,1,0:T(8,128)(2,1)} %l_in.1, bf16[2,48,768]{2,1,0:T(8,128)(2,1)} %b_in.1, bf16[2,8,768]{2,1,0:T(8,128)(2,1)} %a_in.1, bf16[128,128]{1,0:T(8,128)(2,1)} %z_in.1), custom_call_target="tpu_custom_call" | custom-call | tf_op jit(solution)/shard_map/selected_inverse/pallas_call | solution.py:783
  127.3 0.0 copy-start
  127.3 1.7 %copy.8 = f32[2,48,768]{2,1,0:T(8,128)} copy(f32[2,48,768]{2,1,0:T(8,128)} %get-tuple-element.4) | data formatting | bytes 589824
  129.0 0.0 copy-done
  129.0 0.6 copy.9
Async XLA Ops:
  127.3 1.7 %copy-start = (f32[2,8,768]{2,1,0:T(8,128)S(1)}, f32[2,8,768]{2,1,0:T(8,128)}, u32[]{:S(2)}) copy-start(f32[2,8,768]{2,1,0:T(8,128)} %get-tuple-element.5) | copy-start | bytes 147460

commit v6 on v5

--- a/solution.py
+++ b/solution.py
@@ -314,7 +314,6 @@
     q_tile[EVEN] = even[panel + arrow:].astype(F32)
     m_tile[ODD] = odd_far[c, panel:panel + arrow].astype(F32)
     q_tile[ODD] = odd_far[c, panel + arrow:].astype(F32)
-    odd_cols.start()
     even_cols.wait()
     odd_panel.wait()
     new_map(lambda k: odd_far[k, :panel + arrow], EVEN, PAIR)
@@ -416,6 +415,7 @@
         for d in FAN:
             fan_copy(d, 1).start()
         pair_cols.start()
+        odd_cols.start()
         pair_rows.start()
         pair_cols.wait()
         pair_rows.wait()
@@ -456,6 +456,7 @@
         def _():
             scan_cols[2].start()
 
+        odd_cols.start()
         plane.finish(PAIR, PLANE)
         z_each([z_diag(n) for n in (3, 2, 1)], lambda move: move.start())
 

time: 130 us -> 129 us (level)
  Pallas kernels: 127 us -> 125 us
where the time goes in v6:
time: 129 us; the launch traced here: 128 us
  Pallas kernels  125 us (97%)
  local copies, waits for them, and re-layouts  2.33 us (2%)
    pallas_call x1, Pallas kernels, on_device(): pl.pallas_call(functools.partial(kernel, planes, (row, node, panel, own_a...  125 us

profile of v6, /device:TPU:32, one launch (start us, length us, event | category | flops | bytes accessed | tf_op | source)
XLA Modules:
  0.0 128.3 jit_solution(17484346716341044185)
XLA Ops:
  0.6 125.4 %selected_inverse.1 = (f32[2,48,768]{2,1,0:T(8,128)}, f32[2,8,768]{2,1,0:T(8,128)}) custom-call(bf16[2,48,768]{2,1,0:T(8,128)(2,1)} %l_in.1, bf16[2,48,768]{2,1,0:T(8,128)(2,1)} %b_in.1, bf16[2,8,768]{2,1,0:T(8,128)(2,1)} %a_in.1, bf16[128,128]{1,0:T(8,128)(2,1)} %z_in.1), custom_call_target="tpu_custom_call" | custom-call | tf_op jit(solution)/shard_map/selected_inverse/pallas_call | solution.py:784
  126.0 0.0 copy-start
  126.0 1.7 %copy.8 = f32[2,48,768]{2,1,0:T(8,128)} copy(f32[2,48,768]{2,1,0:T(8,128)} %get-tuple-element.4) | data formatting | bytes 589824
  127.7 0.0 copy-done
  127.7 0.6 copy.9
Async XLA Ops:
  126.0 1.7 %copy-start = (f32[2,8,768]{2,1,0:T(8,128)S(1)}, f32[2,8,768]{2,1,0:T(8,128)}, u32[]{:S(2)}) copy-start(f32[2,8,768]{2,1,0:T(8,128)} %get-tuple-element.5) | copy-start | bytes 147460

commit v7 on v6

--- a/solution.py
+++ b/solution.py
@@ -428,6 +428,7 @@
         new_map(lambda k: far_map[0, k], PAIR, PLANE)
         z_each([z_map(0)], lambda move: move.start())
         scan_cols[1].start()
+        scan_rows[1].start()
         pair.finish(EVEN, PAIR)
 
         @pl.when(has[1])
@@ -435,7 +436,6 @@
             z_map(0)[1].wait_recv()
             far_maps[1].start()
 
-        scan_rows[1].start()
         pair_rows.wait()
         fan_wait(1)
         plane.start(lambda k: far_diag[0, k], PAIR)

time: 129 us -> 131 us (1.016)
  Pallas kernels: 125 us -> 127 us
where the time goes in v7:
time: 131 us; the launch traced here: 130 us
  Pallas kernels  127 us (97%)
  local copies, waits for them, and re-layouts  2.33 us (2%)
    pallas_call x1, Pallas kernels, on_device(): pl.pallas_call(functools.partial(kernel, planes, (row, node, panel, own_a...  127 us

profile of v7, /device:TPU:32, one launch (start us, length us, event | category | flops | bytes accessed | tf_op | source)
XLA Modules:
  0.0 129.5 jit_solution(17341242727860443282)
XLA Ops:
  0.6 126.6 %selected_inverse.1 = (f32[2,48,768]{2,1,0:T(8,128)}, f32[2,8,768]{2,1,0:T(8,128)}) custom-call(bf16[2,48,768]{2,1,0:T(8,128)(2,1)} %l_in.1, bf16[2,48,768]{2,1,0:T(8,128)(2,1)} %b_in.1, bf16[2,8,768]{2,1,0:T(8,128)(2,1)} %a_in.1, bf16[128,128]{1,0:T(8,128)(2,1)} %z_in.1), custom_call_target="tpu_custom_call" | custom-call | tf_op jit(solution)/shard_map/selected_inverse/pallas_call | solution.py:784
  127.2 0.0 copy-start
  127.2 1.7 %copy.8 = f32[2,48,768]{2,1,0:T(8,128)} copy(f32[2,48,768]{2,1,0:T(8,128)} %get-tuple-element.4) | data formatting | bytes 589824
  128.9 0.0 copy-done
  128.9 0.6 copy.9
Async XLA Ops:
  127.2 1.7 %copy-start = (f32[2,8,768]{2,1,0:T(8,128)S(1)}, f32[2,8,768]{2,1,0:T(8,128)}, u32[]{:S(2)}) copy-start(f32[2,8,768]{2,1,0:T(8,128)} %get-tuple-element.5) | copy-start | bytes 147460
